TPU v7x, 1024 devices: a whole 4x8x16 slice. The times are simulated.
1024 devices in a mesh: clus: 64 (over y, x, core), sub: 16 (over z).
Axes of the slice: x: 4, y: 8, z: 16, core: 2. Of those that a mesh axis runs over, the one named last changes fastest.
Arguments:
- schur: bfloat16 [64, 16, 512, 512], P('clus', 'sub'), as said below
- load: float32 [64, 16, 4, 16, 128], P('clus', 'sub')
- rigid: float32 [64, 16, 4, 6, 128], P('clus', 'sub')
- lengths: int32 [64, 16, 4], P('clus', 'sub'), may hold values from 0 to 128, as said below
- partner: int32 [64, 16, 4, 128], P('clus', 'sub'), may hold values from 0 to 127, as said below
- coarse_inverse: float32 [384, 384], replicated, as said below
Outputs:
- multipliers: float32 [64, 16, 4, 16, 128], P('clus', 'sub')
- residual: float32 [64, 16, 4, 16, 128], P('clus', 'sub')
Inputs may be any that keep to these rules, and one draw needn't show every extreme that they name: `schur`: each subdomain's matrix is symmetric. `coarse_inverse`: symmetric. `lengths`: both sides of a neighbour pair hold the same length; 0 exactly where no neighbour exists; some pair has 128. On used rows, partner maps the used rows of a pair one to one onto the neighbour's used rows of the opposite direction, and the neighbour's partner maps them back; unused rows hold their own index.
All inputs are finite; a program needn't handle non-finite values.
Results may differ from a plain program's by a relative error of at most 0.0039.
Values sent between devices are 32-bit elements; how exact they have to be, the bound alone decides.
A program may use at most 32 MiB of HBM per device.

v0:
```python
import jax
import jax.numpy as jnp
from jax import lax
from jax.sharding import PartitionSpec as P

ITERS = 2


FULL_PRECISION = lax.Precision.HIGHEST


def extended(block, sides, width):
    for axis, dim in sides:
        count = lax.axis_size(axis)
        forward = [(i, i + 1) for i in range(count - 1)]
        backward = [(target, source) for source, target in forward]
        low = lax.ppermute(
            lax.slice_in_dim(block, block.shape[dim] - width, None, axis=dim), axis, forward
        )
        high = lax.ppermute(lax.slice_in_dim(block, 0, width, axis=dim), axis, backward)
        block = jnp.concatenate([low, block, high], axis=dim)
    return block


def partner_rows(values, table):
    return jnp.einsum("djq,dkq->djk", values, table, precision=FULL_PRECISION)


def across(values, table):
    sub_rim = extended(values[0:2], (("sub", 0),), 1)
    clus_rim = extended(values[2:4], (("clus", 0),), 1)
    arrived = jnp.stack([sub_rim[0], sub_rim[3], clus_rim[0], clus_rim[3]])
    return partner_rows(arrived, table)


def coarse_reduce(local_part):
    within = lax.psum(local_part, "sub")
    return lax.all_gather(within[None], "clus", axis=0, tiled=True)


def inner_total(partial_value):
    return lax.psum(partial_value, ("clus", "sub"))


def half_dot(left_vec, right_vec):
    return 0.5 * jnp.sum(left_vec * right_vec, axis=(0, 2))


def shards(schur, load, rigid, lengths, partner, coarse_inverse):
    own_load = load[0, 0]
    case_count = own_load.shape[1]
    pair_rows = own_load.shape[2]
    rig_own = rigid[0, 0]
    mode_count = rig_own.shape[1]
    column_ids = lax.broadcasted_iota(jnp.int32, (4, pair_rows, pair_rows), 2)
    partner_map = (partner[0, 0][:, :, None] == column_ids).astype(jnp.float32)
    matrix = schur[0, 0]
    blocks = matrix.reshape(4, pair_rows, 4, pair_rows)
    clusters = lax.axis_size("clus")
    cluster_at = lax.axis_index("clus")
    slot_index = lax.broadcasted_iota(jnp.int32, (4, pair_rows), 1)
    live_rows = (slot_index < lengths[0, 0][:, None]).astype(jnp.float32)
    sign_table = jnp.array([-1.0, 1.0, -1.0, 1.0], jnp.float32)
    sign_live = (sign_table[:, None] * live_rows)[:, None, :]
    diag_own = jnp.diagonal(matrix).astype(jnp.float32).reshape(4, 1, pair_rows)
    signed_rigid = rig_own * sign_live
    arrived = across(jnp.concatenate([own_load, diag_own], axis=1), partner_map)

    def expand(coeffs):
        own_coeff = lax.dynamic_index_in_dim(coeffs, cluster_at, 0, keepdims=False)
        near_part = jnp.einsum("dmp,mj->djp", rig_own, own_coeff, precision=FULL_PRECISION)
        return sign_live * (near_part - across(near_part, partner_map))

    dual_rhs = sign_live * (own_load - arrived[:, :case_count])
    weight = live_rows[:, None, :] / (diag_own + arrived[:, case_count : case_count + 1])

    def coarse_local(vector):
        return jnp.einsum("dmp,djp->mj", signed_rigid, vector, precision=FULL_PRECISION)

    def coarse_solve(gathered):
        flattened = gathered.reshape(clusters * mode_count, case_count)
        coeffs = jnp.dot(coarse_inverse, flattened, precision=FULL_PRECISION)
        return coeffs.reshape(clusters, mode_count, case_count)

    multipliers = jnp.zeros_like(own_load)
    residual = dual_rhs
    direction = jnp.zeros_like(own_load)
    rho_old = jnp.ones((case_count,), jnp.float32)
    for iteration in range(ITERS):
        projected = residual - expand(coarse_solve(coarse_reduce(coarse_local(residual))))
        scaled = weight * projected
        precond = scaled - expand(coarse_solve(coarse_reduce(coarse_local(scaled))))
        rho_now = inner_total(half_dot(projected, precond))
        if iteration == 0:
            direction = precond
        else:
            direction = precond + (rho_now / rho_old)[:, None] * direction
        operand = (sign_live * direction).astype(jnp.bfloat16)
        image_rows = jnp.einsum(
            "dcp,dpeq->ecq", operand, blocks, preferred_element_type=jnp.float32
        )
        image_rows = sign_live * (image_rows - across(image_rows, partner_map))
        step_size = rho_now / inner_total(half_dot(direction, image_rows))
        multipliers = multipliers + step_size[:, None] * direction
        residual = residual - step_size[:, None] * image_rows
        rho_old = rho_now
    return (multipliers[None, None], residual[None, None])


def solution(mesh):
    in_specs = (
        P("clus", "sub", None, None),
        P("clus", "sub", None, None, None),
        P("clus", "sub", None, None, None),
        P("clus", "sub", None),
        P("clus", "sub", None, None),
        P(),
    )
    out_specs = (P("clus", "sub", None, None, None), P("clus", "sub", None, None, None))
    return jax.shard_map(shards, mesh=mesh, in_specs=in_specs, out_specs=out_specs, check_vma=False)
```

profile of v0, /device:TPU:1, one launch (start us, length us, event | category | flops | bytes accessed | tf_op | source)
XLA Modules:
  0.0 766.4 jit_solution(4140477828216951726)
XLA Ops:
  0.7 8.1 %gather_fusion = bf16[512]{0:T(512)(128)(2,1)S(1)} fusion(bf16[512,512]{1,0:T(8,128)(2,1)} %bitcast.87, s32[512]{0:T(512)S(1)} %bitcast.86), kind=kCustom, calls=%fused_computation | custom fusion | bytes 6144 | tf_op jit(solution)/shard_map/jit(diagonal)/cond/branch_0_fun/gather | solution.py:65
  8.8 4.8 collective-permute-start
  13.7 1.3 collective-permute-start.1
  15.0 12.5 %collective-permute-start.3 = (f32[1,17,128]{2,1,0:T(8,128)S(1)}, f32[1,17,128]{2,1,0:T(8,128)S(1)}, u32[]{:S(2)}, u32[]{:S(2)}) collective-permute-start(f32[1,17,128]{2,1,0:T(8,128)S(1)} %get-tuple-element.8), channel_id=1, source_target_pairs={{16,0},{32,16},{48,32},{64,48},{80,64},{96,80},{112,96},{128,112},... | collective-permute-start | bytes 26120 | tf_op jit(solution)/shard_map/ppermute | solution.py:20
  27.5 1.9 collective-permute-start.2
  29.6 1.0 collective-permute-done.2
  30.6 0.4 fusion.12
  31.1 27.7 %psum.56 = f32[1,6,16]{2,1,0:T(8,128)S(1)} all-reduce(f32[1,6,16]{2,1,0:T(8,128)S(1)} %convolution_bitcast_fusion.13), channel_id=1, replica_groups=mesh['clus'=64,'sub'=16] {'sub'}, use_global_device_ids=true, to_apply=%region_0.1 | all-reduce | flops 96 | bytes 768 | tf_op jit(solution)/shard_map/psum | solution.py:37
  58.8 51.6 %all_gather.12 = f32[64,6,16]{2,1,0:T(8,128)S(1)} all-gather(f32[1,6,16]{2,1,0:T(8,128)S(1)} %psum.56), channel_id=1, replica_groups=mesh['clus'=64,'sub'=16] {'clus'}, dimensions={0}, use_global_device_ids=true | all-gather | bytes 24960 | tf_op jit(solution)/shard_map/all_gather | solution.py:38
  110.4 0.7 convolution_bitcast_fusion.9
  111.4 0.2 convolution_bitcast_fusion.3
  111.6 1.3 collective-permute-start.4
  112.9 1.9 collective-permute-start.7
  114.9 3.6 collective-permute-start.6
  118.5 1.3 collective-permute-start.5
  119.9 3.0 collective-permute-done.5
  122.9 0.4 fusion.9
  123.4 22.1 %psum.57 = f32[1,6,16]{2,1,0:T(8,128)S(1)} all-reduce(f32[1,6,16]{2,1,0:T(8,128)S(1)} %convolution_bitcast_fusion.12), channel_id=1, replica_groups=mesh['clus'=64,'sub'=16] {'sub'}, use_global_device_ids=true, to_apply=%region_1.2 | all-reduce | flops 96 | bytes 768 | tf_op jit(solution)/shard_map/psum | solution.py:37
  145.6 45.4 %all_gather.13 = f32[64,6,16]{2,1,0:T(8,128)S(1)} all-gather(f32[1,6,16]{2,1,0:T(8,128)S(1)} %psum.57), channel_id=1, replica_groups=mesh['clus'=64,'sub'=16] {'clus'}, dimensions={0}, use_global_device_ids=true | all-gather | bytes 24960 | tf_op jit(solution)/shard_map/all_gather | solution.py:38
  191.0 0.7 convolution_bitcast_fusion.8
  191.9 0.2 convolution_bitcast_fusion.2
  192.2 2.5 collective-permute-start.8
  194.7 2.2 collective-permute-start.11
  196.9 3.4 collective-permute-start.10
  200.3 1.3 collective-permute-start.9
  201.7 2.9 collective-permute-done.9
  204.7 0.4 fusion.7
  205.2 2.2 collective-permute-start.12
  207.4 2.4 collective-permute-start.15
  209.8 3.2 collective-permute-start.14
  213.0 1.3 collective-permute-start.13
  214.3 4.0 collective-permute-done.13
  218.4 0.5 multiply_reduce_fusion.2
  218.9 124.4 %all-reduce = (f32[16]{0:T(128)S(1)}, f32[16]{0:T(128)S(1)}) all-reduce(f32[16]{0:T(128)S(1)} %get-tuple-element.42, f32[16]{0:T(128)S(1)} %get-tuple-element.41), channel_id=1, replica_groups=mesh['clus'=64,'sub'=16] {'clus','sub'}, use_global_device_ids=true, to_apply=%region_3.4 | all-reduce | flops 32 | bytes 256 | tf_op jit(solution)/shard_map/psum | solution.py:42
  343.5 20.5 %psum.60 = f32[1,6,16]{2,1,0:T(8,128)S(1)} all-reduce(f32[1,6,16]{2,1,0:T(8,128)S(1)} %convolution_bitcast_fusion.11), channel_id=1, replica_groups=mesh['clus'=64,'sub'=16] {'sub'}, use_global_device_ids=true, to_apply=%region_6.7 | all-reduce | flops 96 | bytes 768 | tf_op jit(solution)/shard_map/psum | solution.py:37
  364.1 48.1 %all_gather.14 = f32[64,6,16]{2,1,0:T(8,128)S(1)} all-gather(f32[1,6,16]{2,1,0:T(8,128)S(1)} %psum.60), channel_id=1, replica_groups=mesh['clus'=64,'sub'=16] {'clus'}, dimensions={0}, use_global_device_ids=true | all-gather | bytes 24960 | tf_op jit(solution)/shard_map/all_gather | solution.py:38
  412.2 0.7 convolution_bitcast_fusion.7
  413.2 0.2 convolution_bitcast_fusion.1
  413.4 3.1 collective-permute-start.16
  416.6 2.2 collective-permute-start.19
  418.7 3.4 collective-permute-start.18
  422.1 1.3 collective-permute-start.17
  423.5 3.1 collective-permute-done.17
  426.5 0.4 fusion.4
  427.1 21.7 %psum.61 = f32[1,6,16]{2,1,0:T(8,128)S(1)} all-reduce(f32[1,6,16]{2,1,0:T(8,128)S(1)} %convolution_bitcast_fusion.10), channel_id=1, replica_groups=mesh['clus'=64,'sub'=16] {'sub'}, use_global_device_ids=true, to_apply=%region_7.8 | all-reduce | flops 96 | bytes 768 | tf_op jit(solution)/shard_map/psum | solution.py:37
  448.8 46.5 %all_gather.15 = f32[64,6,16]{2,1,0:T(8,128)S(1)} all-gather(f32[1,6,16]{2,1,0:T(8,128)S(1)} %psum.61), channel_id=1, replica_groups=mesh['clus'=64,'sub'=16] {'clus'}, dimensions={0}, use_global_device_ids=true | all-gather | bytes 24960 | tf_op jit(solution)/shard_map/all_gather | solution.py:38
  495.4 0.7 convolution_bitcast_fusion.6
  496.3 0.2 convolution_bitcast_fusion
  496.6 2.5 collective-permute-start.20
  499.1 2.2 collective-permute-start.23
  501.3 3.4 collective-permute-start.22
  504.7 1.3 collective-permute-start.21
  506.0 3.1 collective-permute-done.21
  509.1 0.5 multiply_reduce_fusion.1
  509.6 122.3 %psum.62 = f32[16]{0:T(128)S(1)} all-reduce(f32[16]{0:T(128)S(1)} %broadcast_multiply_fusion.2), channel_id=1, replica_groups=mesh['clus'=64,'sub'=16] {'clus','sub'}, use_global_device_ids=true, to_apply=%region_9.10 | all-reduce | flops 16 | bytes 128 | tf_op jit(solution)/shard_map/psum | solution.py:42
  631.9 0.2 convolution_bitcast_fusion.4
  632.2 1.3 collective-permute-start.24
  633.5 2.6 collective-permute-start.27
  636.0 3.0 collective-permute-start.26
  639.0 1.3 collective-permute-start.25
  640.4 3.3 collective-permute-done.25
  643.6 0.5 multiply_reduce_fusion
  644.1 121.5 %psum.63 = f32[16]{0:T(128)S(1)} all-reduce(f32[16]{0:T(128)S(1)} %broadcast_multiply_fusion.1), channel_id=1, replica_groups=mesh['clus'=64,'sub'=16] {'clus','sub'}, use_global_device_ids=true, to_apply=%region_11.12 | all-reduce | flops 16 | bytes 128 | tf_op jit(solution)/shard_map/psum | solution.py:42
  765.6 0.7 subtract_bitcast_fusion
  (73 shorter events, 2.3 us)
Async XLA Ops:
  0.6 109.8 %copy-start = (f32[384,384]{1,0:T(8,128)S(1)}, f32[384,384]{1,0:T(8,128)}, u32[]{:S(2)}) copy-start(f32[384,384]{1,0:T(8,128)} %param.12) | copy-start | bytes 1769476
  0.7 8.1 %copy-start.3 = (f32[1,1,4,16,128]{4,3,2,1,0:T(8,128)S(1)}, f32[1,1,4,16,128]{4,3,2,1,0:T(8,128)}, u32[]{:S(2)}) copy-start(f32[1,1,4,16,128]{4,3,2,1,0:T(8,128)} %param.8) | copy-start | bytes 98308
  8.8 20.7 %copy-start.4 = (s32[1,1,4]{2,1,0:T(1,128)S(1)}, s32[1,1,4]{2,1,0:T(1,128)}, u32[]{:S(2)}) copy-start(s32[1,1,4]{2,1,0:T(1,128)} %param.10) | copy-start | bytes 52
  8.8 20.6 %copy-start.5 = (f32[4]{0:T(128)S(1)}, f32[4]{0:T(128)}, u32[]{:S(2)}) copy-start(f32[4]{0:T(128)} %constant.30.clone) | copy-start | bytes 52
  8.8 20.7 %copy-start.2 = (f32[1,1,4,6,128]{4,2,3,1,0:T(4,128)S(1)}, f32[1,1,4,6,128]{4,2,3,1,0:T(4,128)}, u32[]{:S(2)}) copy-start(f32[1,1,4,6,128]{4,2,3,1,0:T(4,128)} %param.9) | copy-start | bytes 36868
  8.8 20.7 %collective-permute-start = (f32[1,17,128]{2,1,0:T(8,128)S(1)}, f32[1,17,128]{2,1,0:T(8,128)S(1)}, u32[]{:S(2)}, u32[]{:S(2)}) collective-permute-start(f32[1,17,128]{2,1,0:T(8,128)S(1)} %get-tuple-element.6), channel_id=1, source_target_pairs={{0,1},{1,2},{2,3},{3,4},{4,5},{5,6},{6,7},{7,8},{8,9},{9,10},{10,1... | collective-permute-start | bytes 26120 | tf_op jit(solution)/shard_map/ppermute | solution.py:17
  13.7 15.9 %collective-permute-start.1 = (f32[1,17,128]{2,1,0:T(8,128)S(1)}, f32[1,17,128]{2,1,0:T(8,128)S(1)}, u32[]{:S(2)}, u32[]{:S(2)}) collective-permute-start(f32[1,17,128]{2,1,0:T(8,128)S(1)} %get-tuple-element.7), channel_id=1, source_target_pairs={{1,0},{2,1},{3,2},{4,3},{5,4},{6,5},{7,6},{8,7},{9,8},{10,9},{11,1... | collective-permute-start | bytes 26120 | tf_op jit(solution)/shard_map/ppermute | solution.py:20
  15.0 14.6 %collective-permute-start.3 = (f32[1,17,128]{2,1,0:T(8,128)S(1)}, f32[1,17,128]{2,1,0:T(8,128)S(1)}, u32[]{:S(2)}, u32[]{:S(2)}) collective-permute-start(f32[1,17,128]{2,1,0:T(8,128)S(1)} %get-tuple-element.8), channel_id=1, source_target_pairs={{16,0},{32,16},{48,32},{64,48},{80,64},{96,80},{112,96},{128,112},... | collective-permute-start | bytes 26120 | tf_op jit(solution)/shard_map/ppermute | solution.py:20
  27.5 3.1 collective-permute-start.2
  29.6 1.0 copy-start.6
  111.6 8.3 %collective-permute-start.4 = (f32[1,16,128]{2,1,0:T(8,128)S(1)}, f32[1,16,128]{2,1,0:T(8,128)S(1)}, u32[]{:S(2)}, u32[]{:S(2)}) collective-permute-start(f32[1,16,128]{2,1,0:T(8,128)S(1)} %get-tuple-element.30), channel_id=1, source_target_pairs={{0,1},{1,2},{2,3},{3,4},{4,5},{5,6},{6,7},{7,8},{8,9},{9,10},{10,1... | collective-permute-start | bytes 24584 | tf_op jit(solution)/shard_map/ppermute | solution.py:17
  112.9 7.0 collective-permute-start.7
  114.9 5.0 collective-permute-start.6
  118.5 4.4 collective-permute-start.5
  191.7 9.9 %copy-start.1 = (bf16[1,1,512,512]{3,2,1,0:T(8,128)(2,1)S(1)}, bf16[1,1,512,512]{3,2,1,0:T(8,128)(2,1)}, u32[]{:S(2)}) copy-start(bf16[1,1,512,512]{3,2,1,0:T(8,128)(2,1)} %param.7) | copy-start | bytes 1572868
  192.2 9.5 %collective-permute-start.8 = (f32[1,16,128]{2,1,0:T(8,128)S(1)}, f32[1,16,128]{2,1,0:T(8,128)S(1)}, u32[]{:S(2)}, u32[]{:S(2)}) collective-permute-start(f32[1,16,128]{2,1,0:T(8,128)S(1)} %get-tuple-element.26), channel_id=1, source_target_pairs={{0,1},{1,2},{2,3},{3,4},{4,5},{5,6},{6,7},{7,8},{8,9},{9,10},{10,1... | collective-permute-start | bytes 24584 | tf_op jit(solution)/shard_map/ppermute | solution.py:17
  194.7 7.0 collective-permute-start.11
  196.9 4.9 collective-permute-start.10
  200.3 4.4 collective-permute-start.9
  205.2 9.1 %collective-permute-start.12 = (f32[1,16,128]{2,1,0:T(8,128)S(1)}, f32[1,16,128]{2,1,0:T(8,128)S(1)}, u32[]{:S(2)}, u32[]{:S(2)}) collective-permute-start(f32[1,16,128]{2,1,0:T(8,128)S(1)} %get-tuple-element.22), channel_id=1, source_target_pairs={{0,1},{1,2},{2,3},{3,4},{4,5},{5,6},{6,7},{7,8},{8,9},{9,10},{10,1... | collective-permute-start | bytes 24584 | tf_op jit(solution)/shard_map/ppermute | solution.py:17
  207.4 6.9 collective-permute-start.15
  209.8 4.5 collective-permute-start.14
  213.0 5.4 collective-permute-start.13
  413.4 10.0 %collective-permute-start.16 = (f32[1,16,128]{2,1,0:T(8,128)S(1)}, f32[1,16,128]{2,1,0:T(8,128)S(1)}, u32[]{:S(2)}, u32[]{:S(2)}) collective-permute-start(f32[1,16,128]{2,1,0:T(8,128)S(1)} %get-tuple-element.18), channel_id=1, source_target_pairs={{0,1},{1,2},{2,3},{3,4},{4,5},{5,6},{6,7},{7,8},{8,9},{9,10},{10,1... | collective-permute-start | bytes 24584 | tf_op jit(solution)/shard_map/ppermute | solution.py:17
  416.6 6.9 collective-permute-start.19
  418.7 4.7 collective-permute-start.18
  422.1 4.4 collective-permute-start.17
  496.6 9.4 %collective-permute-start.20 = (f32[1,16,128]{2,1,0:T(8,128)S(1)}, f32[1,16,128]{2,1,0:T(8,128)S(1)}, u32[]{:S(2)}, u32[]{:S(2)}) collective-permute-start(f32[1,16,128]{2,1,0:T(8,128)S(1)} %get-tuple-element.14), channel_id=1, source_target_pairs={{0,1},{1,2},{2,3},{3,4},{4,5},{5,6},{6,7},{7,8},{8,9},{9,10},{10,1... | collective-permute-start | bytes 24584 | tf_op jit(solution)/shard_map/ppermute | solution.py:17
  499.1 6.9 collective-permute-start.23
  501.3 4.7 collective-permute-start.22
  504.7 4.4 collective-permute-start.21
  632.2 8.2 %collective-permute-start.24 = (f32[1,16,128]{2,1,0:T(8,128)S(1)}, f32[1,16,128]{2,1,0:T(8,128)S(1)}, u32[]{:S(2)}, u32[]{:S(2)}) collective-permute-start(f32[1,16,128]{2,1,0:T(8,128)S(1)} %get-tuple-element.10), channel_id=1, source_target_pairs={{0,1},{1,2},{2,3},{3,4},{4,5},{5,6},{6,7},{7,8},{8,9},{9,10},{10,1... | collective-permute-start | bytes 24584 | tf_op jit(solution)/shard_map/ppermute | solution.py:17
  633.5 6.9 collective-permute-start.27
  636.0 4.3 collective-permute-start.26
  639.0 4.6 collective-permute-start.25
where the time goes:
time: 770 us; the launch traced here: 766 us
  blocking collectives  652 us (85%)
  starting transfers between devices  74.6 us (10%)
  waiting for transfers between devices  20.4 us (3%)
  local copies, waits for them, and re-layouts  9.22 us (1%)
  matrix products  7.77 us (1%)
    psum x3, blocking collectives, inner_total(): return lax.psum(partial_value, ('clus', 'sub'))  368 us
    all_gather x4, blocking collectives, coarse_reduce(): return lax.all_gather(within[None], 'clus', axis=0, tiled=True)  192 us
    psum x4, blocking collectives, coarse_reduce(): within = lax.psum(local_part, 'sub')  92.1 us
    ppermute x14, starting transfers between devices, extended(): lax.ppermute(lax.slice_in_dim(block, block.shape[dim] - width, None, axis...  39.6 us
    ppermute x14, starting transfers between devices, extended(): lax.ppermute(lax.slice_in_dim(block, 0, width, axis=dim), axis, backward)  35 us
    ppermute x14, waiting for transfers between devices, extended(): lax.ppermute(lax.slice_in_dim(block, 0, width, axis=dim), axis, backward)  19.4 us
  transfers between devices with their start and end apart: 28, of which 7 were waited for; matrix products, arithmetic and copies ran while one was open for 0% of the time, Pallas kernels for 0%

commit v1 on v0

v1 whole, which is shorter than its diff:
```python
import functools

import jax
import jax.numpy as jnp
from jax import lax
from jax.experimental import pallas as pl
from jax.experimental.pallas import tpu as pltpu
from jax.sharding import PartitionSpec as P

MESH = pl.DeviceIdType.MESH
HIGHEST = lax.Precision.HIGHEST
F32 = jnp.float32

NCL, NSUB, CHIPS = 64, 16, 32
CASES, MODES, PAIR = 16, 6, 128
ROWS = 4 * PAIR
SIGNS = (-1.0, 1.0, -1.0, 1.0)


def nn(a, b):
    return lax.dot_general(a, b, (((1,), (0,)), ((), ())), precision=HIGHEST, preferred_element_type=F32)


def nt(a, b):
    return lax.dot_general(a, b, (((1,), (1,)), ((), ())), precision=HIGHEST, preferred_element_type=F32)


def tn(a, b):
    return lax.dot_general(a, b, (((0,), (0,)), ((), ())), precision=HIGHEST, preferred_element_type=F32)


def iota(shape, dim):
    return lax.broadcasted_iota(jnp.int32, shape, dim)


def join(parts):
    return jnp.concatenate(parts, axis=1)


def tile4(x):
    return join([x, x, x, x])


def kernel(
    schur_ref, load_ref, rigid_ref, len_ref, partner_ref, inv_ref, mult_ref, res_ref,
    mat, inv, padded, coupling, edge, edge_in, halo, halo_in, halo2, halo2_in,
    out1, z1_in, g1, out2, z2_in, g2, out3, z3_in, mid3, x3_in, core3, core3_in,
    in_sem, halo_send, halo_recv, tree_send, tree_recv,
):
    c, s = lax.axis_index("clus"), lax.axis_index("sub")
    core, chip = lax.rem(c, 2), lax.div(c, 2)

    z_peers = [(c, lax.rem(s + o, NSUB)) for o in range(1, NSUB)]
    plane = [(lax.rem(chip + o, CHIPS) * 2 + core, s) for o in range(1, CHIPS)]
    other = (chip * 2 + 1 - core, s)
    near = [
        (c, lax.rem(s + NSUB - 1, NSUB)),
        (c, lax.rem(s + 1, NSUB)),
        (lax.rem(c + NCL - 1, NCL), s),
        (lax.rem(c + 1, NCL), s),
    ]
    away = (lax.rem(c + NCL - 1 + 2 * core, NCL), s)
    greeted = z_peers + plane + [other, away]

    barrier = pltpu.get_barrier_semaphore()
    for peer in greeted:
        pl.semaphore_signal(barrier, inc=1, device_id=peer, device_id_type=MESH)

    loads = [
        pltpu.make_async_copy(schur_ref.at[0, 0], mat, in_sem.at[0]),
        pltpu.make_async_copy(load_ref.at[0, 0], edge.at[:, pl.ds(0, CASES)], in_sem.at[1]),
        pltpu.make_async_copy(rigid_ref.at[0, 0], edge.at[:, pl.ds(CASES, MODES)], in_sem.at[2]),
        pltpu.make_async_copy(inv_ref, inv, in_sem.at[3]),
    ]
    for copy in loads:
        copy.start()

    def send_all(src, dst_of, peers, stage):
        for i, peer in enumerate(peers):
            pltpu.make_async_remote_copy(
                src_ref=src, dst_ref=dst_of(i), send_sem=tree_send.at[stage], recv_sem=tree_recv.at[stage],
                device_id=peer, device_id_type=MESH,
            ).start()

    def whole(ref, stage, peer):
        return pltpu.make_async_remote_copy(
            src_ref=ref, dst_ref=ref, send_sem=tree_send.at[stage], recv_sem=tree_recv.at[stage],
            device_id=peer, device_id_type=MESH,
        )

    def halo_copies(src, dst, which):
        return [
            pltpu.make_async_remote_copy(
                src_ref=src.at[d], dst_ref=dst.at[d ^ 1], send_sem=halo_send.at[which, d],
                recv_sem=halo_recv.at[which, d ^ 1], device_id=near[d], device_id_type=MESH,
            )
            for d in range(4)
        ]

    coupling[...] = jnp.zeros((512, 512), F32)
    lane = iota((1, PAIR), 1)
    live_parts = [(lane < len_ref[0, 0, d]).astype(F32) for d in range(4)]
    live = join(live_parts)
    sign_live = join([SIGNS[d] * live_parts[d] for d in range(4)])
    index = [partner_ref[0, 0, pl.ds(d, 1), :] for d in range(4)]

    def partner_rows(x, d):
        return jnp.take_along_axis(x, jnp.broadcast_to(index[d], x.shape), axis=1)

    loads[0].wait()
    eye = iota((PAIR, PAIR), 0) == iota((PAIR, PAIR), 1)
    for d in range(4):
        block = mat[pl.ds(d * PAIR, PAIR), pl.ds(d * PAIR, PAIR)].astype(F32)
        diag = jnp.sum(jnp.where(eye, block, 0.0), axis=0, keepdims=True)
        edge[d, pl.ds(CASES + MODES, 2), :] = jnp.concatenate([diag, jnp.zeros((1, PAIR), F32)], axis=0)
    loads[1].wait()
    loads[2].wait()
    loads[3].wait()
    spread_row, spread_col = iota((512, 384), 0), iota((512, 384), 1)
    slot = spread_row & 7
    spread = jnp.where((slot < MODES) & ((spread_row >> 3) * MODES + slot == spread_col), 1.0, 0.0).astype(F32)
    padded[pl.ds(0, 8), :] = jnp.zeros((8, 512), F32)
    padded[pl.ds(520, 8), :] = jnp.zeros((8, 512), F32)
    padded[pl.ds(8, 512), :] = nt(nn(spread, inv[...]), spread)

    pl.semaphore_wait(barrier, len(greeted))
    edge_copies = halo_copies(edge, edge_in, 0)
    for copy in edge_copies:
        copy.start()

    mode_row = iota((8, PAIR), 0) < MODES
    own = [edge[d] for d in range(4)]
    own_load = join([x[0:CASES] for x in own])
    own_rigid = join([jnp.where(mode_row, x[CASES:], 0.0) for x in own])
    own_diag = join([x[CASES + MODES : CASES + MODES + 1] for x in own])
    signed_rigid = sign_live * own_rigid
    inv3 = padded[pl.ds(pl.multiple_of(c * 8, 8), 24), :]

    for copy in edge_copies:
        copy.wait_recv()
    met = [partner_rows(edge_in[d], d) for d in range(4)]
    far_load = join([x[0:CASES] for x in met])
    far_rigid = [jnp.where(mode_row, x[CASES:], 0.0) for x in met]
    far_diag = join([x[CASES + MODES : CASES + MODES + 1] for x in met])
    weight = jnp.where(live > 0.0, 1.0 / (own_diag + far_diag), 0.0)
    nil = jnp.zeros((8, PAIR), F32)
    rhs = sign_live * (own_load - far_load)
    spread_own = sign_live * (own_rigid - join([far_rigid[0], far_rigid[1], nil, nil]))
    spread_low = -sign_live * join([nil, nil, far_rigid[2], nil])
    spread_high = -sign_live * join([nil, nil, nil, far_rigid[3]])
    basis = jnp.concatenate([spread_low, spread_own, spread_high], axis=0)

    weighted_rhs = weight * rhs
    first = jnp.concatenate([rhs, weighted_rhs, weight * basis, jnp.zeros((72, ROWS), F32)], axis=0)
    sums = nt(signed_rigid, first)
    row8 = iota((8, PAIR), 0)
    packed = sums + pltpu.roll(pltpu.roll(sums, 64, 1), 5, 0)
    out1[...] = packed[0:3]
    send_all(out1, lambda i: z1_in.at[i, pl.ds(0, 3)], z_peers, 0)
    wide1 = sign_live * basis
    signed3 = jnp.concatenate(
        [part for k in range(3) for part in (wide1[8 * k : 8 * k + 8], weight * wide1[8 * k : 8 * k + 8])], axis=0
    )
    whole(z1_in.at[:, pl.ds(0, 3)], 0, z_peers[0]).wait_recv()
    total = out1[...]
    for i in range(NSUB - 1):
        total = total + z1_in[i, pl.ds(0, 3), :]
    g1[core, chip, pl.ds(0, 3), :] = total
    mine1 = g1.at[core, chip, pl.ds(0, 3)]
    send_all(mine1, lambda i: mine1, plane, 1)
    rest1 = g1.at[core, pl.ds(0, CHIPS - 1), pl.ds(0, 3)]
    whole(rest1, 1, plane[0]).wait_recv()
    half1 = g1.at[core, :, pl.ds(0, 3)]
    send_all(half1, lambda i: half1, [other], 2)
    whole(half1, 2, other).wait_recv()

    lane8 = iota((8, PAIR), 1)
    stacked = []
    for k in range(NCL):
        part = jnp.concatenate([g1[k % 2, k // 2, pl.ds(0, 3), :], jnp.zeros((5, PAIR), F32)], axis=0)
        part = part + pltpu.roll(pltpu.roll(part, 64, 1), 3, 0)
        stacked.append(part)
        column = 8 * (k - 1)
        moved = pltpu.roll(part, (column - 32) % PAIR, 1)
        tiles = sorted({(column + 8 * e) // PAIR for e in range(3) if 0 <= k - 1 + e < NCL})
        for t in tiles:
            first_lane = max(column, 0) - t * PAIR
            last_lane = min(column + 24, ROWS) - t * PAIR
            keep = (lane8 >= first_lane) & (lane8 < last_lane)
            coupling[pl.ds(8 * k, 8), pl.ds(t * PAIR, PAIR)] = jnp.where(keep, moved, 0.0)
    gathered = jnp.concatenate(stacked, axis=0)
    twice = nn(nn(inv3, coupling[...]), padded[pl.ds(8, 512), :])
    solver = jnp.concatenate([inv3, twice], axis=0)

    def solve(sums512):
        y = nn(solver, sums512)
        return join([y[0:24, 0:CASES], y[0:24, CASES : 2 * CASES] - y[24:48, 0:CASES]])

    def project(vector, coeffs):
        e = tn(coeffs, basis)
        projected = vector - e[0:CASES]
        return projected, weight * projected - e[CASES:]

    projected, direction = project(rhs, solve(gathered))
    ones = jnp.ones((8, ROWS), F32)
    operand = sign_live * direction
    image = jnp.dot(operand.astype(jnp.bfloat16), mat[...], preferred_element_type=F32)

    image_sums = nt(signed3, image)
    scalars = nt(ones, jnp.concatenate([0.5 * projected * direction, operand * image], axis=0))
    lanes2 = join([image_sums[8 * k : 8 * k + 8] for k in range(6)] + [scalars])
    out2[...] = lanes2[0:6]
    send_all(out2, lambda i: z2_in.at[i, pl.ds(0, 6)], z_peers, 3)
    for d in range(4):
        halo[d] = image[:, d * PAIR : (d + 1) * PAIR]
    image_copies = halo_copies(halo, halo_in, 1)
    for copy in image_copies:
        copy.start()
    whole(z2_in.at[:, pl.ds(0, 6)], 3, z_peers[0]).wait_recv()
    total = out2[...]
    for i in range(NSUB - 1):
        total = total + z2_in[i, pl.ds(0, 6), :]
    g2[core, chip, pl.ds(0, 6), :] = total
    mine2 = g2.at[core, chip, pl.ds(0, 6)]
    send_all(mine2, lambda i: mine2, plane, 4)
    for copy in image_copies:
        copy.wait_recv()
    applied = sign_live * (image - join([partner_rows(halo_in[d], d) for d in range(4)]))
    rest2 = g2.at[core, pl.ds(0, CHIPS - 1), pl.ds(0, 6)]
    whole(rest2, 4, plane[0]).wait_recv()
    half2 = g2.at[core, :, pl.ds(0, 6)]
    send_all(half2, lambda i: half2, [other], 5)
    whole(half2, 5, other).wait_recv()

    parts = [
        jnp.concatenate([g2[k % 2, k // 2, pl.ds(0, 6), :], jnp.zeros((2, PAIR), F32)], axis=0) for k in range(NCL)
    ]
    shifted = []
    for k in range(NCL):
        x = pltpu.roll(parts[k], PAIR - 32, 1)
        if k + 1 < NCL:
            x = x + parts[k + 1]
        if k > 0:
            x = x + pltpu.roll(parts[k - 1], PAIR - 64, 1)
        shifted.append(x)
    sums_all = parts[0]
    for k in range(1, NCL):
        sums_all = sums_all + parts[k]

    def column(row, start, count):
        pick = jnp.where(iota((count * CASES, PAIR), 1) == iota((count * CASES, PAIR), 0) + start, 1.0, 0.0)
        return nt(pick.astype(F32), jnp.broadcast_to(row, (PAIR, PAIR)))

    both = column(sums_all[0:1], 96, 2)
    rho, curve = both[0:CASES], both[CASES:]
    step = tile4(rho / curve)
    projected_f, direction_f = project(applied, solve(jnp.concatenate(shifted, axis=0)))
    projected1 = projected - step * projected_f
    precond1 = direction - step * direction_f
    operand1 = sign_live * precond1
    high = operand1.astype(jnp.bfloat16)
    low = (operand1 - high.astype(F32)).astype(jnp.bfloat16)
    image2 = jnp.dot(jnp.concatenate([high, low], axis=0), mat[...], preferred_element_type=F32)
    image1 = image2[0:CASES] + image2[CASES:]

    scalars3 = nt(
        ones,
        jnp.concatenate(
            [
                0.5 * projected1 * precond1,
                operand1 * image1,
                operand1 * image + operand * image1,
                jnp.zeros((80, ROWS), F32),
            ],
            axis=0,
        ),
    )
    out3[...] = scalars3[0:1]
    send_all(out3, lambda i: z3_in.at[pl.ds(i, 1)], z_peers, 6)
    for d in range(4):
        halo2[d] = image1[:, d * PAIR : (d + 1) * PAIR]
    image_copies1 = halo_copies(halo2, halo2_in, 2)
    for copy in image_copies1:
        copy.start()
    multipliers = step * direction
    residual1 = rhs - step * applied
    whole(z3_in, 6, z_peers[0]).wait_recv()
    mid3[...] = out3[...] + jnp.sum(z3_in[...], axis=0, keepdims=True)
    send_all(mid3, lambda i: x3_in.at[pl.ds(i, 1)], plane, 7)
    for copy in image_copies1:
        copy.wait_recv()
    applied1 = sign_live * (image1 - join([partner_rows(halo2_in[d], d) for d in range(4)]))
    whole(x3_in, 7, plane[0]).wait_recv()
    core3[...] = mid3[...] + jnp.sum(x3_in[...], axis=0, keepdims=True)
    send_all(core3, lambda i: core3_in, [other], 8)
    whole(core3_in, 8, other).wait_recv()
    tail = column(core3[...] + core3_in[...], 0, 3)
    rho1, square, cross = tail[0:CASES], tail[CASES : 2 * CASES], tail[2 * CASES :]
    beta = rho1 / rho
    step1 = tile4(rho1 / (square + beta * cross + beta * beta * curve))
    beta = tile4(beta)
    multipliers = multipliers + step1 * (precond1 + beta * direction)
    residual = residual1 - step1 * (applied1 + beta * applied)
    for d in range(4):
        mult_ref[0, 0, d] = multipliers[:, d * PAIR : (d + 1) * PAIR]
        res_ref[0, 0, d] = residual[:, d * PAIR : (d + 1) * PAIR]

    for copy in edge_copies + image_copies + image_copies1:
        copy.wait_send()
    whole(z1_in.at[:, pl.ds(0, 3)], 0, z_peers[0]).wait_send()
    whole(rest1, 1, plane[0]).wait_send()
    whole(half1, 2, other).wait_send()
    whole(z2_in.at[:, pl.ds(0, 6)], 3, z_peers[0]).wait_send()
    whole(rest2, 4, plane[0]).wait_send()
    whole(half2, 5, other).wait_send()
    whole(z3_in, 6, z_peers[0]).wait_send()
    whole(x3_in, 7, plane[0]).wait_send()
    whole(core3_in, 8, other).wait_send()


def shards(schur, load, rigid, lengths, partner, coarse_inverse):
    anywhere = pl.BlockSpec(memory_space=pl.ANY)
    vmem = pl.BlockSpec(memory_space=pltpu.VMEM)
    out = jax.ShapeDtypeStruct(load.shape, F32)
    return pl.pallas_call(
        kernel,
        out_shape=(out, out),
        in_specs=[anywhere, anywhere, anywhere, pl.BlockSpec(memory_space=pltpu.SMEM), vmem, anywhere],
        out_specs=(vmem, vmem),
        scratch_shapes=[
            pltpu.VMEM((ROWS, ROWS), jnp.bfloat16),
            pltpu.VMEM((384, 384), F32),
            pltpu.VMEM((528, 512), F32),
            pltpu.VMEM((512, 512), F32),
            pltpu.VMEM((4, 24, PAIR), F32),
            pltpu.VMEM((4, 24, PAIR), F32),
            pltpu.VMEM((4, CASES, PAIR), F32),
            pltpu.VMEM((4, CASES, PAIR), F32),
            pltpu.VMEM((4, CASES, PAIR), F32),
            pltpu.VMEM((4, CASES, PAIR), F32),
            pltpu.VMEM((3, PAIR), F32),
            pltpu.VMEM((NSUB - 1, 8, PAIR), F32),
            pltpu.VMEM((2, CHIPS, 8, PAIR), F32),
            pltpu.VMEM((6, PAIR), F32),
            pltpu.VMEM((NSUB - 1, 8, PAIR), F32),
            pltpu.VMEM((2, CHIPS, 8, PAIR), F32),
            pltpu.VMEM((1, PAIR), F32),
            pltpu.VMEM((NSUB - 1, PAIR), F32),
            pltpu.VMEM((1, PAIR), F32),
            pltpu.VMEM((CHIPS - 1, PAIR), F32),
            pltpu.VMEM((1, PAIR), F32),
            pltpu.VMEM((1, PAIR), F32),
            pltpu.SemaphoreType.DMA((4,)),
            pltpu.SemaphoreType.DMA((3, 4)),
            pltpu.SemaphoreType.DMA((3, 4)),
            pltpu.SemaphoreType.DMA((9,)),
            pltpu.SemaphoreType.DMA((9,)),
        ],
        compiler_params=pltpu.CompilerParams(
            collective_id=0, has_side_effects=True, vmem_limit_bytes=32 * 1024 * 1024
        ),
        name="feti",
    )(schur, load, rigid, lengths, partner, coarse_inverse)


def solution(mesh):
    in_specs = (
        P("clus", "sub", None, None),
        P("clus", "sub", None, None, None),
        P("clus", "sub", None, None, None),
        P("clus", "sub", None),
        P("clus", "sub", None, None),
        P(),
    )
    out_specs = (P("clus", "sub", None, None, None), P("clus", "sub", None, None, None))
    return jax.shard_map(shards, mesh=mesh, in_specs=in_specs, out_specs=out_specs, check_vma=False)
```

time: 770 us -> 82.3 us (0.11)
  blocking collectives: 652 us -> 0 us
  Pallas kernels: 0 us -> 76.5 us
  starting transfers between devices: 74.6 us -> 0 us
  waiting for transfers between devices: 20.4 us -> 0 us
  matrix products: 7.77 us -> 0 us
    psum x7 -> x0, blocking collectives: 460 us -> none  [the longest x3 368 us: inner_total(): return lax.psum(partial_value, ('clus', 'sub'))]
    all_gather x4 -> x0, blocking collectives: 192 us -> none  [coarse_reduce(): return lax.all_gather(within[None], 'clus', axis=0, tiled=True)]
    pallas_call x0 -> x1, Pallas kernels: none -> 76.5 us  [shards(): pl.pallas_call(kernel, out_shape=(out, out), in_specs=[anywhere, anywhere...]
    ppermute x28 -> x0, starting transfers between devices: 74.6 us -> none  [the longest x14 39.6 us: extended(): lax.ppermute(lax.slice_in_dim(block, block.shape[dim] - width, None, axis...]
    ppermute x28 -> x0, waiting for transfers between devices: 20.4 us -> none  [the longest x14 19.4 us: extended(): lax.ppermute(lax.slice_in_dim(block, 0, width, axis=dim), axis, backward)]
    gather x1 -> x0, local copies, waits for them, and re-layouts: 8.09 us -> none  [shards(): diag_own = jnp.diagonal(matrix).astype(jnp.float32).reshape(4, 1, pair_rows)]
    dot_general x21 -> x0, matrix products: 7.77 us -> none  [the longest x7 2.99 us: partner_rows(): return jnp.einsum('djq,dkq->djk', values, table, precision=FULL_PRECISION)]
  transfers between devices with their start and end apart: 28 -> 0, of which waited for: 7 -> 0; matrix products, arithmetic and copies ran while one was open for 0% -> 0% of each run, Pallas kernels for 0% -> 0%
where the time goes in v1:
time: 82.3 us; the launch traced here: 82 us
  Pallas kernels  76.5 us (93%)
  local copies, waits for them, and re-layouts  4.82 us (6%)
    pallas_call x1, Pallas kernels, shards(): pl.pallas_call(kernel, out_shape=(out, out), in_specs=[anywhere, anywhere...  76.5 us
    unnamed x13, local copies, waits for them, and re-layouts  4.82 us

profile of v1, /device:TPU:1, one launch (start us, length us, event | category | flops | bytes accessed | tf_op | source)
XLA Modules:
  0.0 82.0 jit_solution(4693075013352016122)
XLA Ops:
  0.6 0.0 copy-start.3
  0.6 0.0 copy-start.4
  0.7 0.7 copy.8.rigid_ref
  1.4 0.0 copy-done.3
  1.4 0.0 copy-done.4
  1.4 0.0 copy-start
  1.4 1.1 %copy-done = f32[384,384]{1,0:T(8,128)S(1)} copy-done((f32[384,384]{1,0:T(8,128)S(1)}, f32[384,384]{1,0:T(8,128)}, u32[]{:S(2)}) %copy-start) | copy-done | bytes 589848
  2.4 0.0 copy-start.1
  2.4 1.0 %copy-done.1 = bf16[1,1,512,512]{3,2,1,0:T(8,128)(2,1)S(1)} copy-done((bf16[1,1,512,512]{3,2,1,0:T(8,128)(2,1)S(1)}, bf16[1,1,512,512]{3,2,1,0:T(8,128)(2,1)}, u32[]{:S(2)}) %copy-start.1) | copy-done | bytes 524312
  3.5 0.0 copy-start.2
  3.5 0.8 copy-done.2
  4.2 76.5 %feti.1 = (f32[1,1,4,16,128]{4,3,2,1,0:T(8,128)S(1)}, f32[1,1,4,16,128]{4,3,2,1,0:T(8,128)S(1)}) custom-call(bf16[1,1,512,512]{3,2,1,0:T(8,128)(2,1)S(1)} %copy-done.1, f32[1,1,4,16,128]{4,3,2,1,0:T(8,128)S(1)} %copy-done.2, f32[1,1,4,6,128]{4,3,2,1,0:T(8,128)S(1)} %copy.8.rigid_ref, s32[1,1,4]{2,1,0:T(1,128)S(1)} %copy-done.4, ...), custom_call_target="tpu_custom_call" | custom-call | tf_op jit(solution)/shard_map/feti/pallas_call | solution.py:325
  80.7 0.6 copy.11
  81.4 0.6 copy.12
Async XLA Ops:
  0.6 0.7 copy-start.3
  0.6 0.7 copy-start.4
  1.4 1.1 %copy-start = (f32[384,384]{1,0:T(8,128)S(1)}, f32[384,384]{1,0:T(8,128)}, u32[]{:S(2)}) copy-start(f32[384,384]{1,0:T(8,128)} %inv_ref.1) | copy-start | bytes 1769476
  2.4 1.0 %copy-start.1 = (bf16[1,1,512,512]{3,2,1,0:T(8,128)(2,1)S(1)}, bf16[1,1,512,512]{3,2,1,0:T(8,128)(2,1)}, u32[]{:S(2)}) copy-start(bf16[1,1,512,512]{3,2,1,0:T(8,128)(2,1)} %schur_ref.1) | copy-start | bytes 1572868
  3.5 0.8 copy-start.2

commit v2 on v1

--- a/solution.py
+++ b/solution.py
@@ -42,16 +42,18 @@
 
 
 def kernel(
-    schur_ref, load_ref, rigid_ref, len_ref, partner_ref, inv_ref, mult_ref, res_ref,
-    mat, inv, padded, coupling, edge, edge_in, halo, halo_in, halo2, halo2_in,
+    schur_ref, load_ref, rigid_ref, len_ref, partner_ref, inv_ref, both_ref,
+    mat, inv, used, rows_of, padded, coupling, edge, edge_in, halo, halo_in, halo2, halo2_in,
     out1, z1_in, g1, out2, z2_in, g2, out3, z3_in, mid3, x3_in, core3, core3_in,
     in_sem, halo_send, halo_recv, tree_send, tree_recv,
 ):
     c, s = lax.axis_index("clus"), lax.axis_index("sub")
     core, chip = lax.rem(c, 2), lax.div(c, 2)
 
-    z_peers = [(c, lax.rem(s + o, NSUB)) for o in range(1, NSUB)]
-    plane = [(lax.rem(chip + o, CHIPS) * 2 + core, s) for o in range(1, CHIPS)]
+    z_peers = [(c, lax.rem(s + o, NSUB)) for o in sorted(range(1, NSUB), key=lambda o: -min(o, NSUB - o))]
+    y, x = lax.div(chip, 4), lax.rem(chip, 4)
+    steps = sorted(range(1, CHIPS), key=lambda o: -(min(o // 4, 8 - o // 4) + min(o % 4, 4 - o % 4)))
+    plane = [((lax.rem(y + o // 4, 8) * 4 + lax.rem(x + o % 4, 4)) * 2 + core, s) for o in steps]
     other = (chip * 2 + 1 - core, s)
     near = [
         (c, lax.rem(s + NSUB - 1, NSUB)),
@@ -67,12 +69,16 @@
         pl.semaphore_signal(barrier, inc=1, device_id=peer, device_id_type=MESH)
 
     loads = [
-        pltpu.make_async_copy(schur_ref.at[0, 0], mat, in_sem.at[0]),
-        pltpu.make_async_copy(load_ref.at[0, 0], edge.at[:, pl.ds(0, CASES)], in_sem.at[1]),
-        pltpu.make_async_copy(rigid_ref.at[0, 0], edge.at[:, pl.ds(CASES, MODES)], in_sem.at[2]),
-        pltpu.make_async_copy(inv_ref, inv, in_sem.at[3]),
+        pltpu.make_async_copy(load_ref.at[0, 0], edge.at[:, pl.ds(0, CASES)], in_sem.at[0]),
+        pltpu.make_async_copy(schur_ref.at[0, 0], mat, in_sem.at[1]),
+        pltpu.make_async_copy(len_ref.at[0], used, in_sem.at[2]),
+        pltpu.make_async_copy(partner_ref.at[0, 0], rows_of, in_sem.at[3]),
+        pltpu.make_async_copy(inv_ref, inv, in_sem.at[4]),
+    ] + [
+        pltpu.make_async_copy(rigid_ref.at[0, 0, :, d], edge.at[d, pl.ds(CASES, MODES)], in_sem.at[5 + d])
+        for d in range(4)
     ]
-    for copy in loads:
+    for copy in loads[0:2] + loads[5:] + loads[2:5]:
         copy.start()
 
     def send_all(src, dst_of, peers, stage):
@@ -97,44 +103,37 @@
             for d in range(4)
         ]
 
-    coupling[...] = jnp.zeros((512, 512), F32)
-    lane = iota((1, PAIR), 1)
-    live_parts = [(lane < len_ref[0, 0, d]).astype(F32) for d in range(4)]
-    live = join(live_parts)
-    sign_live = join([SIGNS[d] * live_parts[d] for d in range(4)])
-    index = [partner_ref[0, 0, pl.ds(d, 1), :] for d in range(4)]
-
-    def partner_rows(x, d):
-        return jnp.take_along_axis(x, jnp.broadcast_to(index[d], x.shape), axis=1)
-
-    loads[0].wait()
+    loads[1].wait()
     eye = iota((PAIR, PAIR), 0) == iota((PAIR, PAIR), 1)
     for d in range(4):
         block = mat[pl.ds(d * PAIR, PAIR), pl.ds(d * PAIR, PAIR)].astype(F32)
         diag = jnp.sum(jnp.where(eye, block, 0.0), axis=0, keepdims=True)
         edge[d, pl.ds(CASES + MODES, 2), :] = jnp.concatenate([diag, jnp.zeros((1, PAIR), F32)], axis=0)
-    loads[1].wait()
-    loads[2].wait()
-    loads[3].wait()
-    spread_row, spread_col = iota((512, 384), 0), iota((512, 384), 1)
-    slot = spread_row & 7
-    spread = jnp.where((slot < MODES) & ((spread_row >> 3) * MODES + slot == spread_col), 1.0, 0.0).astype(F32)
-    padded[pl.ds(0, 8), :] = jnp.zeros((8, 512), F32)
-    padded[pl.ds(520, 8), :] = jnp.zeros((8, 512), F32)
-    padded[pl.ds(8, 512), :] = nt(nn(spread, inv[...]), spread)
-
+    for copy in loads[0:1] + loads[5:]:
+        copy.wait()
     pl.semaphore_wait(barrier, len(greeted))
     edge_copies = halo_copies(edge, edge_in, 0)
     for copy in edge_copies:
         copy.start()
 
+    for copy in loads[2:4]:
+        copy.wait()
+    lane = iota((1, PAIR), 1)
+    live_parts = [(lane < jnp.broadcast_to(used[:, d : d + 1], (1, PAIR))).astype(F32) for d in range(4)]
+    live = join(live_parts)
+    sign_live = join([SIGNS[d] * live_parts[d] for d in range(4)])
+    index = [rows_of[pl.ds(d, 1), :] for d in range(4)]
+
+    def partner_rows(x, d):
+        return jnp.take_along_axis(x, jnp.broadcast_to(index[d], x.shape), axis=1)
+
+    coupling[...] = jnp.zeros((512, 512), F32)
     mode_row = iota((8, PAIR), 0) < MODES
     own = [edge[d] for d in range(4)]
     own_load = join([x[0:CASES] for x in own])
     own_rigid = join([jnp.where(mode_row, x[CASES:], 0.0) for x in own])
     own_diag = join([x[CASES + MODES : CASES + MODES + 1] for x in own])
     signed_rigid = sign_live * own_rigid
-    inv3 = padded[pl.ds(pl.multiple_of(c * 8, 8), 24), :]
 
     for copy in edge_copies:
         copy.wait_recv()
@@ -161,6 +160,14 @@
     signed3 = jnp.concatenate(
         [part for k in range(3) for part in (wide1[8 * k : 8 * k + 8], weight * wide1[8 * k : 8 * k + 8])], axis=0
     )
+    loads[4].wait()
+    spread_row, spread_col = iota((512, 384), 0), iota((512, 384), 1)
+    slot = spread_row & 7
+    spread = jnp.where((slot < MODES) & ((spread_row >> 3) * MODES + slot == spread_col), 1.0, 0.0).astype(F32)
+    padded[pl.ds(0, 8), :] = jnp.zeros((8, 512), F32)
+    padded[pl.ds(520, 8), :] = jnp.zeros((8, 512), F32)
+    padded[pl.ds(8, 512), :] = nt(nn(spread, inv[...]), spread)
+    inv3 = padded[pl.ds(pl.multiple_of(c * 8, 8), 24), :]
     whole(z1_in.at[:, pl.ds(0, 3)], 0, z_peers[0]).wait_recv()
     total = out1[...]
     for i in range(NSUB - 1):
@@ -302,8 +309,8 @@
     multipliers = multipliers + step1 * (precond1 + beta * direction)
     residual = residual1 - step1 * (applied1 + beta * applied)
     for d in range(4):
-        mult_ref[0, 0, d] = multipliers[:, d * PAIR : (d + 1) * PAIR]
-        res_ref[0, 0, d] = residual[:, d * PAIR : (d + 1) * PAIR]
+        both_ref[0, d] = multipliers[:, d * PAIR : (d + 1) * PAIR]
+        both_ref[1, d] = residual[:, d * PAIR : (d + 1) * PAIR]
 
     for copy in edge_copies + image_copies + image_copies1:
         copy.wait_send()
@@ -319,17 +326,19 @@
 
 
 def shards(schur, load, rigid, lengths, partner, coarse_inverse):
-    anywhere = pl.BlockSpec(memory_space=pl.ANY)
+    hbm = pl.BlockSpec(memory_space=pl.ANY)
     vmem = pl.BlockSpec(memory_space=pltpu.VMEM)
-    out = jax.ShapeDtypeStruct(load.shape, F32)
-    return pl.pallas_call(
+    out = jax.ShapeDtypeStruct((2,) + load.shape[2:], F32)
+    both = pl.pallas_call(
         kernel,
-        out_shape=(out, out),
-        in_specs=[anywhere, anywhere, anywhere, pl.BlockSpec(memory_space=pltpu.SMEM), vmem, anywhere],
-        out_specs=(vmem, vmem),
+        out_shape=out,
+        in_specs=[hbm] * 6,
+        out_specs=vmem,
         scratch_shapes=[
             pltpu.VMEM((ROWS, ROWS), jnp.bfloat16),
             pltpu.VMEM((384, 384), F32),
+            pltpu.VMEM((1, 4), jnp.int32),
+            pltpu.VMEM((4, PAIR), jnp.int32),
             pltpu.VMEM((528, 512), F32),
             pltpu.VMEM((512, 512), F32),
             pltpu.VMEM((4, 24, PAIR), F32),
@@ -350,17 +359,18 @@
             pltpu.VMEM((CHIPS - 1, PAIR), F32),
             pltpu.VMEM((1, PAIR), F32),
             pltpu.VMEM((1, PAIR), F32),
-            pltpu.SemaphoreType.DMA((4,)),
+            pltpu.SemaphoreType.DMA((9,)),
             pltpu.SemaphoreType.DMA((3, 4)),
             pltpu.SemaphoreType.DMA((3, 4)),
             pltpu.SemaphoreType.DMA((9,)),
             pltpu.SemaphoreType.DMA((9,)),
         ],
         compiler_params=pltpu.CompilerParams(
-            collective_id=0, has_side_effects=True, vmem_limit_bytes=32 * 1024 * 1024
+            collective_id=0, has_side_effects=True, vmem_limit_bytes=60 * 1024*1024
         ),
         name="feti",
-    )(schur, load, rigid, lengths, partner, coarse_inverse)
+    )(schur, load, jnp.transpose(rigid, (0, 1, 3, 2, 4)), lengths, partner, coarse_inverse)
+    return both[0][None, None], both[1][None, None]
 
 
 def solution(mesh):

time: 82.3 us -> 76.8 us (0.933)
  local copies, waits for them, and re-layouts: 4.82 us -> 1.4 us
  Pallas kernels: 76.5 us -> 74.5 us
    unnamed x13 -> x0, local copies, waits for them, and re-layouts: 4.82 us -> none
    pallas_call x1, Pallas kernels: 76.5 us -> 74.5 us  [shards(): pl.pallas_call(kernel, out_shape=out, in_specs=[hbm] * 6, out_specs=vmem,...]
    another operation x0 -> x1, local copies, waits for them, and re-layouts: none -> 1.4 us  [shards(): return (both[0][None, None], both[1][None, None])]
where the time goes in v2:
time: 76.8 us; the launch traced here: 76.5 us
  Pallas kernels  74.5 us (97%)
  local copies, waits for them, and re-layouts  1.4 us (2%)
    pallas_call x1, Pallas kernels, shards(): pl.pallas_call(kernel, out_shape=out, in_specs=[hbm] * 6, out_specs=vmem,...  74.5 us

profile of v2, /device:TPU:1, one launch (start us, length us, event | category | flops | bytes accessed | tf_op | source)
XLA Modules:
  0.0 76.5 jit_solution(10468270719124085928)
XLA Ops:
  0.6 74.5 %feti.1 = f32[2,4,16,128]{3,2,1,0:T(8,128)} custom-call(bf16[1,1,512,512]{3,2,1,0:T(8,128)(2,1)} %schur_ref.1, f32[1,1,4,16,128]{4,3,2,1,0:T(8,128)} %load_ref.1, f32[1,1,6,4,128]{4,3,2,1,0:T(4,128)} %bitcast.5, s32[1,1,4]{2,1,0:T(1,128)} %len_ref.1, s32[1,1,4,128]{3,2,1,0:T(4,128)} %partner_ref.1, f32[384,384]{1,0:T(8,128)} %inv_ref.1), custom_call_target="tpu_custom_call" | custom-call | tf_op jit(solution)/shard_map/feti/pallas_call | solution.py:332
  75.1 1.4 %slice_bitcast_fusion = (f32[1,1,4,16,128]{4,3,2,1,0:T(8,128)}, f32[1,1,4,16,128]{4,3,2,1,0:T(8,128)}) fusion(f32[2,4,16,128]{3,2,1,0:T(8,128)} %feti.1), kind=kLoop, calls=%fused_computation | loop fusion | bytes 131072 | tf_op jit(solution)/shard_map/broadcast_in_dim;squeeze | solution.py:373

commit v3 on v2

--- a/solution.py
+++ b/solution.py
@@ -17,16 +17,39 @@
 SIGNS = (-1.0, 1.0, -1.0, 1.0)
 
 
+def full_dot(a, b, dims):
+    return lax.dot_general(a, b, (dims, ((), ())), precision=HIGHEST, preferred_element_type=F32)
+
+
+def split(x):
+    high = x.astype(jnp.bfloat16).astype(F32)
+    return high, x - high
+
+
+def dot3(a, b, dims):
+    keep = 1 - dims[0][0]
+    count = a.shape[keep]
+    a_high, a_low = split(a)
+    pair = jnp.concatenate([a_high, a_low], axis=keep).astype(jnp.bfloat16)
+    b_high, b_low = b if isinstance(b, tuple) else [x.astype(jnp.bfloat16) for x in split(b)]
+
+    def dot(x, y):
+        return lax.dot_general(x, y, (dims, ((), ())), preferred_element_type=F32)
+
+    both = dot(pair, b_high)
+    return both[:count] + both[count:] + dot(a_high.astype(jnp.bfloat16), b_low)
+
+
 def nn(a, b):
-    return lax.dot_general(a, b, (((1,), (0,)), ((), ())), precision=HIGHEST, preferred_element_type=F32)
+    return dot3(a, b, ((1,), (0,)))
 
 
 def nt(a, b):
-    return lax.dot_general(a, b, (((1,), (1,)), ((), ())), precision=HIGHEST, preferred_element_type=F32)
+    return dot3(a, b, ((1,), (1,)))
 
 
 def tn(a, b):
-    return lax.dot_general(a, b, (((0,), (0,)), ((), ())), precision=HIGHEST, preferred_element_type=F32)
+    return dot3(a, b, ((0,), (0,)))
 
 
 def iota(shape, dim):
@@ -43,9 +66,9 @@
 
 def kernel(
     schur_ref, load_ref, rigid_ref, len_ref, partner_ref, inv_ref, both_ref,
-    mat, inv, used, rows_of, padded, coupling, edge, edge_in, halo, halo_in, halo2, halo2_in,
+    mat, corner, inv, used, rows_of, padded, padded_high, padded_low, coupling, edge, edge_in, halo, halo_in, halo2, halo2_in,
     out1, z1_in, g1, out2, z2_in, g2, out3, z3_in, mid3, x3_in, core3, core3_in,
-    in_sem, halo_send, halo_recv, tree_send, tree_recv,
+    in_sem, halo_send, halo_recv, tree_send, tree_recv, ready,
 ):
     c, s = lax.axis_index("clus"), lax.axis_index("sub")
     core, chip = lax.rem(c, 2), lax.div(c, 2)
@@ -62,7 +85,33 @@
         (lax.rem(c + 1, NCL), s),
     ]
     away = (lax.rem(c + NCL - 1 + 2 * core, NCL), s)
-    greeted = z_peers + plane + [other, away]
+
+    def z_by(o):
+        return (c, lax.rem(s + o + NSUB, NSUB))
+
+    def y_by(o):
+        return ((lax.rem(y + o + 8, 8) * 4 + x) * 2 + core, s)
+
+    def x_by(o):
+        return ((y * 4 + lax.rem(x + o + 4, 4)) * 2 + core, s)
+
+    greeted = [z_by(-1), z_by(1), y_by(-1), y_by(1), x_by(-1), x_by(1), other, away]
+    told = [
+        [z_by(-1), z_by(1)],
+        [z_by(-2), z_by(2)],
+        [z_by(-4), z_by(4)],
+        [x_by(-1), x_by(1)],
+        [y_by(-1), y_by(1)],
+        [y_by(-2), y_by(2)],
+        [y_by(-1), y_by(1)],
+    ]
+
+    def tell(k):
+        for peer in told[k]:
+            pl.semaphore_signal(ready.at[k], inc=1, device_id=peer, device_id_type=MESH)
+
+    def hear(k):
+        pl.semaphore_wait(ready.at[k], 2)
 
     barrier = pltpu.get_barrier_semaphore()
     for peer in greeted:
@@ -74,11 +123,18 @@
         pltpu.make_async_copy(len_ref.at[0], used, in_sem.at[2]),
         pltpu.make_async_copy(partner_ref.at[0, 0], rows_of, in_sem.at[3]),
         pltpu.make_async_copy(inv_ref, inv, in_sem.at[4]),
-    ] + [
+    ]
+    rigid_loads = [
         pltpu.make_async_copy(rigid_ref.at[0, 0, :, d], edge.at[d, pl.ds(CASES, MODES)], in_sem.at[5 + d])
         for d in range(4)
     ]
-    for copy in loads[0:2] + loads[5:] + loads[2:5]:
+    corner_loads = [
+        pltpu.make_async_copy(
+            schur_ref.at[0, 0, pl.ds(d * PAIR, PAIR), pl.ds(d * PAIR, PAIR)], corner.at[d], in_sem.at[9 + d]
+        )
+        for d in range(4)
+    ]
+    for copy in corner_loads + rigid_loads + loads[0:1] + loads[2:4] + loads[1:2] + loads[4:5]:
         copy.start()
 
     def send_all(src, dst_of, peers, stage):
@@ -103,18 +159,24 @@
             for d in range(4)
         ]
 
-    loads[1].wait()
+    pl.semaphore_wait(barrier, len(greeted))
+    tell(0)
+    tell(3)
     eye = iota((PAIR, PAIR), 0) == iota((PAIR, PAIR), 1)
     for d in range(4):
-        block = mat[pl.ds(d * PAIR, PAIR), pl.ds(d * PAIR, PAIR)].astype(F32)
+        corner_loads[d].wait()
+        block = corner[d].astype(F32)
         diag = jnp.sum(jnp.where(eye, block, 0.0), axis=0, keepdims=True)
         edge[d, pl.ds(CASES + MODES, 2), :] = jnp.concatenate([diag, jnp.zeros((1, PAIR), F32)], axis=0)
-    for copy in loads[0:1] + loads[5:]:
+    for copy in loads[0:1] + rigid_loads:
         copy.wait()
-    pl.semaphore_wait(barrier, len(greeted))
     edge_copies = halo_copies(edge, edge_in, 0)
     for copy in edge_copies:
         copy.start()
+    hear(0)
+    tell(1)
+    hear(3)
+    tell(4)
 
     for copy in loads[2:4]:
         copy.wait()
@@ -135,6 +197,10 @@
     own_diag = join([x[CASES + MODES : CASES + MODES + 1] for x in own])
     signed_rigid = sign_live * own_rigid
 
+    hear(1)
+    tell(2)
+    hear(4)
+    tell(5)
     for copy in edge_copies:
         copy.wait_recv()
     met = [partner_rows(edge_in[d], d) for d in range(4)]
@@ -155,24 +221,30 @@
     row8 = iota((8, PAIR), 0)
     packed = sums + pltpu.roll(pltpu.roll(sums, 64, 1), 5, 0)
     out1[...] = packed[0:3]
+    hear(2)
     send_all(out1, lambda i: z1_in.at[i, pl.ds(0, 3)], z_peers, 0)
     wide1 = sign_live * basis
     signed3 = jnp.concatenate(
         [part for k in range(3) for part in (wide1[8 * k : 8 * k + 8], weight * wide1[8 * k : 8 * k + 8])], axis=0
     )
+    hear(5)
+    tell(6)
+    loads[1].wait()
     loads[4].wait()
     spread_row, spread_col = iota((512, 384), 0), iota((512, 384), 1)
     slot = spread_row & 7
     spread = jnp.where((slot < MODES) & ((spread_row >> 3) * MODES + slot == spread_col), 1.0, 0.0).astype(F32)
     padded[pl.ds(0, 8), :] = jnp.zeros((8, 512), F32)
     padded[pl.ds(520, 8), :] = jnp.zeros((8, 512), F32)
-    padded[pl.ds(8, 512), :] = nt(nn(spread, inv[...]), spread)
+    padded[pl.ds(8, 512), :] = full_dot(full_dot(spread, inv[...], ((1,), (0,))), spread, ((1,), (1,)))
     inv3 = padded[pl.ds(pl.multiple_of(c * 8, 8), 24), :]
+    padded_high[...], padded_low[...] = [part.astype(jnp.bfloat16) for part in split(padded[pl.ds(8, 512), :])]
     whole(z1_in.at[:, pl.ds(0, 3)], 0, z_peers[0]).wait_recv()
     total = out1[...]
     for i in range(NSUB - 1):
         total = total + z1_in[i, pl.ds(0, 3), :]
     g1[core, chip, pl.ds(0, 3), :] = total
+    hear(6)
     mine1 = g1.at[core, chip, pl.ds(0, 3)]
     send_all(mine1, lambda i: mine1, plane, 1)
     rest1 = g1.at[core, pl.ds(0, CHIPS - 1), pl.ds(0, 3)]
@@ -196,7 +268,7 @@
             keep = (lane8 >= first_lane) & (lane8 < last_lane)
             coupling[pl.ds(8 * k, 8), pl.ds(t * PAIR, PAIR)] = jnp.where(keep, moved, 0.0)
     gathered = jnp.concatenate(stacked, axis=0)
-    twice = nn(nn(inv3, coupling[...]), padded[pl.ds(8, 512), :])
+    twice = nn(nn(inv3, coupling[...]), (padded_high[...], padded_low[...]))
     solver = jnp.concatenate([inv3, twice], axis=0)
 
     def solve(sums512):
@@ -256,7 +328,7 @@
 
     def column(row, start, count):
         pick = jnp.where(iota((count * CASES, PAIR), 1) == iota((count * CASES, PAIR), 0) + start, 1.0, 0.0)
-        return nt(pick.astype(F32), jnp.broadcast_to(row, (PAIR, PAIR)))
+        return full_dot(pick.astype(F32), jnp.broadcast_to(row, (PAIR, PAIR)), ((1,), (1,)))
 
     both = column(sums_all[0:1], 96, 2)
     rho, curve = both[0:CASES], both[CASES:]
@@ -336,10 +408,13 @@
         out_specs=vmem,
         scratch_shapes=[
             pltpu.VMEM((ROWS, ROWS), jnp.bfloat16),
+            pltpu.VMEM((4, PAIR, PAIR), jnp.bfloat16),
             pltpu.VMEM((384, 384), F32),
             pltpu.VMEM((1, 4), jnp.int32),
             pltpu.VMEM((4, PAIR), jnp.int32),
             pltpu.VMEM((528, 512), F32),
+            pltpu.VMEM((512, 512), jnp.bfloat16),
+            pltpu.VMEM((512, 512), jnp.bfloat16),
             pltpu.VMEM((512, 512), F32),
             pltpu.VMEM((4, 24, PAIR), F32),
             pltpu.VMEM((4, 24, PAIR), F32),
@@ -359,11 +434,12 @@
             pltpu.VMEM((CHIPS - 1, PAIR), F32),
             pltpu.VMEM((1, PAIR), F32),
             pltpu.VMEM((1, PAIR), F32),
-            pltpu.SemaphoreType.DMA((9,)),
+            pltpu.SemaphoreType.DMA((13,)),
             pltpu.SemaphoreType.DMA((3, 4)),
             pltpu.SemaphoreType.DMA((3, 4)),
             pltpu.SemaphoreType.DMA((9,)),
             pltpu.SemaphoreType.DMA((9,)),
+            pltpu.SemaphoreType.REGULAR((7,)),
         ],
         compiler_params=pltpu.CompilerParams(
             collective_id=0, has_side_effects=True, vmem_limit_bytes=60 * 1024*1024

time: 76.8 us -> 74.8 us (0.974)
  Pallas kernels: 74.5 us -> 72.5 us
    pallas_call x1, Pallas kernels: 74.5 us -> 72.5 us  [shards(): pl.pallas_call(kernel, out_shape=out, in_specs=[hbm] * 6, out_specs=vmem,...]
where the time goes in v3:
time: 74.8 us; the launch traced here: 74.5 us
  Pallas kernels  72.5 us (97%)
  local copies, waits for them, and re-layouts  1.4 us (2%)
    pallas_call x1, Pallas kernels, shards(): pl.pallas_call(kernel, out_shape=out, in_specs=[hbm] * 6, out_specs=vmem,...  72.5 us

profile of v3, /device:TPU:1, one launch (start us, length us, event | category | flops | bytes accessed | tf_op | source)
XLA Modules:
  0.0 74.5 jit_solution(152334352234232457)
XLA Ops:
  0.6 72.5 %feti.1 = f32[2,4,16,128]{3,2,1,0:T(8,128)} custom-call(bf16[1,1,512,512]{3,2,1,0:T(8,128)(2,1)} %schur_ref.1, f32[1,1,4,16,128]{4,3,2,1,0:T(8,128)} %load_ref.1, f32[1,1,6,4,128]{4,3,2,1,0:T(4,128)} %bitcast.5, s32[1,1,4]{2,1,0:T(1,128)} %len_ref.1, s32[1,1,4,128]{3,2,1,0:T(4,128)} %partner_ref.1, f32[384,384]{1,0:T(8,128)} %inv_ref.1), custom_call_target="tpu_custom_call" | custom-call | tf_op jit(solution)/shard_map/feti/pallas_call | solution.py:404
  73.1 1.4 %slice_bitcast_fusion = (f32[1,1,4,16,128]{4,3,2,1,0:T(8,128)}, f32[1,1,4,16,128]{4,3,2,1,0:T(8,128)}) fusion(f32[2,4,16,128]{3,2,1,0:T(8,128)} %feti.1), kind=kLoop, calls=%fused_computation | loop fusion | bytes 131072 | tf_op jit(solution)/shard_map/broadcast_in_dim;squeeze | solution.py:449

commit v4 on v3

--- a/solution.py
+++ b/solution.py
@@ -65,9 +65,9 @@
 
 
 def kernel(
-    schur_ref, load_ref, rigid_ref, len_ref, partner_ref, inv_ref, both_ref,
+    schur_ref, load_ref, rigid_ref, len_ref, partner_ref, inv_ref, terms_ref, step_ref, older_ref, staged,
     mat, corner, inv, used, rows_of, padded, padded_high, padded_low, coupling, edge, edge_in, halo, halo_in, halo2, halo2_in,
-    out1, z1_in, g1, out2, z2_in, g2, out3, z3_in, mid3, x3_in, core3, core3_in,
+    out1, z1_in, g1, out2, z2_in, g2, out3, z3_in, mid3, x3_in,
     in_sem, halo_send, halo_recv, tree_send, tree_recv, ready,
 ):
     c, s = lax.axis_index("clus"), lax.axis_index("sub")
@@ -78,6 +78,14 @@
     steps = sorted(range(1, CHIPS), key=lambda o: -(min(o // 4, 8 - o // 4) + min(o % 4, 4 - o % 4)))
     plane = [((lax.rem(y + o // 4, 8) * 4 + lax.rem(x + o % 4, 4)) * 2 + core, s) for o in steps]
     other = (chip * 2 + 1 - core, s)
+    spans = sorted(
+        range(1, NCL), key=lambda o: -(min(o // 8, 8 - o // 8) + min(o // 2 % 4, 4 - o // 2 % 4) + o % 2)
+    )
+    clusters = [
+        ((lax.rem(y + o // 8, 8) * 4 + lax.rem(x + o // 2 % 4, 4)) * 2 + lax.rem(core + o % 2, 2), s) for o in spans
+    ]
+    columns = sorted(range(1, 2 * NSUB), key=lambda o: -(min(o // 2, NSUB - o // 2) + o % 2))
+    column_peers = [(chip * 2 + lax.rem(core + o, 2), lax.rem(s + o // 2, NSUB)) for o in columns]
     near = [
         (c, lax.rem(s + NSUB - 1, NSUB)),
         (c, lax.rem(s + 1, NSUB)),
@@ -243,20 +251,17 @@
     total = out1[...]
     for i in range(NSUB - 1):
         total = total + z1_in[i, pl.ds(0, 3), :]
-    g1[core, chip, pl.ds(0, 3), :] = total
+    g1[c, pl.ds(0, 3), :] = total
     hear(6)
-    mine1 = g1.at[core, chip, pl.ds(0, 3)]
-    send_all(mine1, lambda i: mine1, plane, 1)
-    rest1 = g1.at[core, pl.ds(0, CHIPS - 1), pl.ds(0, 3)]
-    whole(rest1, 1, plane[0]).wait_recv()
-    half1 = g1.at[core, :, pl.ds(0, 3)]
-    send_all(half1, lambda i: half1, [other], 2)
-    whole(half1, 2, other).wait_recv()
+    mine1 = g1.at[c, pl.ds(0, 3)]
+    send_all(mine1, lambda i: mine1, clusters, 1)
+    rest1 = g1.at[pl.ds(0, NCL - 1), pl.ds(0, 3)]
+    whole(rest1, 1, clusters[0]).wait_recv()
 
     lane8 = iota((8, PAIR), 1)
     stacked = []
     for k in range(NCL):
-        part = jnp.concatenate([g1[k % 2, k // 2, pl.ds(0, 3), :], jnp.zeros((5, PAIR), F32)], axis=0)
+        part = jnp.concatenate([g1[k, pl.ds(0, 3), :], jnp.zeros((5, PAIR), F32)], axis=0)
         part = part + pltpu.roll(pltpu.roll(part, 64, 1), 3, 0)
         stacked.append(part)
         column = 8 * (k - 1)
@@ -299,20 +304,17 @@
     total = out2[...]
     for i in range(NSUB - 1):
         total = total + z2_in[i, pl.ds(0, 6), :]
-    g2[core, chip, pl.ds(0, 6), :] = total
-    mine2 = g2.at[core, chip, pl.ds(0, 6)]
-    send_all(mine2, lambda i: mine2, plane, 4)
+    g2[c, pl.ds(0, 6), :] = total
+    mine2 = g2.at[c, pl.ds(0, 6)]
+    send_all(mine2, lambda i: mine2, clusters, 4)
     for copy in image_copies:
         copy.wait_recv()
     applied = sign_live * (image - join([partner_rows(halo_in[d], d) for d in range(4)]))
-    rest2 = g2.at[core, pl.ds(0, CHIPS - 1), pl.ds(0, 6)]
-    whole(rest2, 4, plane[0]).wait_recv()
-    half2 = g2.at[core, :, pl.ds(0, 6)]
-    send_all(half2, lambda i: half2, [other], 5)
-    whole(half2, 5, other).wait_recv()
+    rest2 = g2.at[pl.ds(0, NCL - 1), pl.ds(0, 6)]
+    whole(rest2, 4, clusters[0]).wait_recv()
 
     parts = [
-        jnp.concatenate([g2[k % 2, k // 2, pl.ds(0, 6), :], jnp.zeros((2, PAIR), F32)], axis=0) for k in range(NCL)
+        jnp.concatenate([g2[k, pl.ds(0, 6), :], jnp.zeros((2, PAIR), F32)], axis=0) for k in range(NCL)
     ]
     shifted = []
     for k in range(NCL):
@@ -355,58 +357,58 @@
         ),
     )
     out3[...] = scalars3[0:1]
-    send_all(out3, lambda i: z3_in.at[pl.ds(i, 1)], z_peers, 6)
+    send_all(out3, lambda i: z3_in.at[pl.ds(i, 1)], column_peers, 6)
     for d in range(4):
         halo2[d] = image1[:, d * PAIR : (d + 1) * PAIR]
     image_copies1 = halo_copies(halo2, halo2_in, 2)
     for copy in image_copies1:
         copy.start()
-    multipliers = step * direction
-    residual1 = rhs - step * applied
-    whole(z3_in, 6, z_peers[0]).wait_recv()
+    def stage(which, *terms):
+        for term, value in enumerate(terms):
+            for d in range(4):
+                staged[term, which, d] = value[:, d * PAIR : (d + 1) * PAIR]
+
+    stage(0, step * direction, precond1, direction)
+    whole(z3_in, 6, column_peers[0]).wait_recv()
     mid3[...] = out3[...] + jnp.sum(z3_in[...], axis=0, keepdims=True)
     send_all(mid3, lambda i: x3_in.at[pl.ds(i, 1)], plane, 7)
     for copy in image_copies1:
         copy.wait_recv()
     applied1 = sign_live * (image1 - join([partner_rows(halo2_in[d], d) for d in range(4)]))
+    stage(1, rhs - step * applied, -applied1, -applied)
+    write_out = pltpu.make_async_copy(staged, terms_ref, in_sem.at[0])
+    write_out.start()
     whole(x3_in, 7, plane[0]).wait_recv()
-    core3[...] = mid3[...] + jnp.sum(x3_in[...], axis=0, keepdims=True)
-    send_all(core3, lambda i: core3_in, [other], 8)
-    whole(core3_in, 8, other).wait_recv()
-    tail = column(core3[...] + core3_in[...], 0, 3)
+    tail = column(mid3[...] + jnp.sum(x3_in[...], axis=0, keepdims=True), 0, 3)
     rho1, square, cross = tail[0:CASES], tail[CASES : 2 * CASES], tail[2 * CASES :]
     beta = rho1 / rho
-    step1 = tile4(rho1 / (square + beta * cross + beta * beta * curve))
-    beta = tile4(beta)
-    multipliers = multipliers + step1 * (precond1 + beta * direction)
-    residual = residual1 - step1 * (applied1 + beta * applied)
-    for d in range(4):
-        both_ref[0, d] = multipliers[:, d * PAIR : (d + 1) * PAIR]
-        both_ref[1, d] = residual[:, d * PAIR : (d + 1) * PAIR]
+    step1 = rho1 / (square + beta * cross + beta * beta * curve)
+    step_ref[...] = step1
+    older_ref[...] = step1 * beta
+    write_out.wait()
 
     for copy in edge_copies + image_copies + image_copies1:
         copy.wait_send()
     whole(z1_in.at[:, pl.ds(0, 3)], 0, z_peers[0]).wait_send()
-    whole(rest1, 1, plane[0]).wait_send()
-    whole(half1, 2, other).wait_send()
+    whole(rest1, 1, clusters[0]).wait_send()
     whole(z2_in.at[:, pl.ds(0, 6)], 3, z_peers[0]).wait_send()
-    whole(rest2, 4, plane[0]).wait_send()
-    whole(half2, 5, other).wait_send()
-    whole(z3_in, 6, z_peers[0]).wait_send()
+    whole(rest2, 4, clusters[0]).wait_send()
+    whole(z3_in, 6, column_peers[0]).wait_send()
     whole(x3_in, 7, plane[0]).wait_send()
-    whole(core3_in, 8, other).wait_send()
 
 
 def shards(schur, load, rigid, lengths, partner, coarse_inverse):
     hbm = pl.BlockSpec(memory_space=pl.ANY)
     vmem = pl.BlockSpec(memory_space=pltpu.VMEM)
-    out = jax.ShapeDtypeStruct((2,) + load.shape[2:], F32)
-    both = pl.pallas_call(
+    terms_out = jax.ShapeDtypeStruct((3, 2) + load.shape[2:], F32)
+    step_out = jax.ShapeDtypeStruct((CASES, PAIR), F32)
+    terms, step, older = pl.pallas_call(
         kernel,
-        out_shape=out,
+        out_shape=(terms_out, step_out, step_out),
         in_specs=[hbm] * 6,
-        out_specs=vmem,
+        out_specs=(hbm, vmem, vmem),
         scratch_shapes=[
+            pltpu.VMEM((3, 2, 4, CASES, PAIR), F32),
             pltpu.VMEM((ROWS, ROWS), jnp.bfloat16),
             pltpu.VMEM((4, PAIR, PAIR), jnp.bfloat16),
             pltpu.VMEM((384, 384), F32),
@@ -424,16 +426,14 @@
             pltpu.VMEM((4, CASES, PAIR), F32),
             pltpu.VMEM((3, PAIR), F32),
             pltpu.VMEM((NSUB - 1, 8, PAIR), F32),
-            pltpu.VMEM((2, CHIPS, 8, PAIR), F32),
+            pltpu.VMEM((NCL, 8, PAIR), F32),
             pltpu.VMEM((6, PAIR), F32),
             pltpu.VMEM((NSUB - 1, 8, PAIR), F32),
-            pltpu.VMEM((2, CHIPS, 8, PAIR), F32),
+            pltpu.VMEM((NCL, 8, PAIR), F32),
             pltpu.VMEM((1, PAIR), F32),
-            pltpu.VMEM((NSUB - 1, PAIR), F32),
+            pltpu.VMEM((2 * NSUB - 1, PAIR), F32),
             pltpu.VMEM((1, PAIR), F32),
             pltpu.VMEM((CHIPS - 1, PAIR), F32),
-            pltpu.VMEM((1, PAIR), F32),
-            pltpu.VMEM((1, PAIR), F32),
             pltpu.SemaphoreType.DMA((13,)),
             pltpu.SemaphoreType.DMA((3, 4)),
             pltpu.SemaphoreType.DMA((3, 4)),
@@ -446,7 +446,9 @@
         ),
         name="feti",
     )(schur, load, jnp.transpose(rigid, (0, 1, 3, 2, 4)), lengths, partner, coarse_inverse)
-    return both[0][None, None], both[1][None, None]
+    return tuple(
+        (terms[0, k] + step[None] * terms[1, k] + older[None] * terms[2, k])[None, None] for k in range(2)
+    )
 
 
 def solution(mesh):

time: 74.8 us -> 72.5 us (0.969)
  Pallas kernels: 72.5 us -> 70.2 us
  other arithmetic: 0 us -> 1.48 us
  local copies, waits for them, and re-layouts: 1.4 us -> 0 us
    pallas_call x1, Pallas kernels: 72.5 us -> 70.2 us  [shards(): pl.pallas_call(kernel, out_shape=(terms_out, step_out, step_out), in_spec...]
    add x0 -> x1, other arithmetic: none -> 1.48 us  [shards(): terms[0, k] + step[None] * terms[1, k] + older[None] * terms[2, k]]
    another operation x1 -> x0, local copies, waits for them, and re-layouts: 1.4 us -> none  [shards(): return (both[0][None, None], both[1][None, None])]
where the time goes in v4:
time: 72.5 us; the launch traced here: 72.3 us
  Pallas kernels  70.2 us (97%)
  other arithmetic  1.48 us (2%)
    pallas_call x1, Pallas kernels, shards(): pl.pallas_call(kernel, out_shape=(terms_out, step_out, step_out), in_spec...  70.2 us
    add x1, other arithmetic, shards(): terms[0, k] + step[None] * terms[1, k] + older[None] * terms[2, k]  1.48 us

profile of v4, /device:TPU:1, one launch (start us, length us, event | category | flops | bytes accessed | tf_op | source)
XLA Modules:
  0.0 72.3 jit_solution(9402534341459703848)
XLA Ops:
  0.6 70.2 %feti.1 = (f32[3,2,4,16,128]{4,3,2,1,0:T(8,128)}, f32[16,128]{1,0:T(8,128)}, f32[16,128]{1,0:T(8,128)}) custom-call(bf16[1,1,512,512]{3,2,1,0:T(8,128)(2,1)} %schur_ref.1, f32[1,1,4,16,128]{4,3,2,1,0:T(8,128)} %load_ref.1, f32[1,1,6,4,128]{4,3,2,1,0:T(4,128)} %bitcast.1, s32[1,1,4]{2,1,0:T(1,128)} %len_ref.1, s32[1,1,4,128]{3,2,1,0:T(4,128)} %partner_ref.1, ...), custom_call_target="tpu_custom_call" | custom-call | tf_op jit(solution)/shard_map/feti/pallas_call | solution.py:405
  70.8 1.5 %multiply_add_fusion = (f32[1,1,4,16,128]{4,3,2,1,0:T(8,128)}, f32[1,1,4,16,128]{4,3,2,1,0:T(8,128)}) fusion(f32[3,2,4,16,128]{4,3,2,1,0:T(8,128)} %get-tuple-element.5, f32[16,128]{1,0:T(8,128)} %get-tuple-element.7, f32[16,128]{1,0:T(8,128)} %get-tuple-element.6), kind=kLoop, calls=%fused_computation | loop fusion | flops 65536 | bytes 278528 | tf_op jit(solution)/shard_map/add | solution.py:450

commit v5 on v4

--- a/solution.py
+++ b/solution.py
@@ -103,10 +103,8 @@
     def x_by(o):
         return ((y * 4 + lax.rem(x + o + 4, 4)) * 2 + core, s)
 
-    greeted = [z_by(-1), z_by(1), y_by(-1), y_by(1), x_by(-1), x_by(1), other, away]
+    greeted = [z_by(o * side) for o in (4, 3, 2, 1) for side in (-1, 1)] + [y_by(-1), y_by(1), x_by(-1), x_by(1), other, away]
     told = [
-        [z_by(-1), z_by(1)],
-        [z_by(-2), z_by(2)],
         [z_by(-4), z_by(4)],
         [x_by(-1), x_by(1)],
         [y_by(-1), y_by(1)],
@@ -169,7 +167,7 @@
 
     pl.semaphore_wait(barrier, len(greeted))
     tell(0)
-    tell(3)
+    tell(1)
     eye = iota((PAIR, PAIR), 0) == iota((PAIR, PAIR), 1)
     for d in range(4):
         corner_loads[d].wait()
@@ -181,10 +179,8 @@
     edge_copies = halo_copies(edge, edge_in, 0)
     for copy in edge_copies:
         copy.start()
-    hear(0)
-    tell(1)
-    hear(3)
-    tell(4)
+    hear(1)
+    tell(2)
 
     for copy in loads[2:4]:
         copy.wait()
@@ -205,10 +201,8 @@
     own_diag = join([x[CASES + MODES : CASES + MODES + 1] for x in own])
     signed_rigid = sign_live * own_rigid
 
-    hear(1)
-    tell(2)
-    hear(4)
-    tell(5)
+    hear(2)
+    tell(3)
     for copy in edge_copies:
         copy.wait_recv()
     met = [partner_rows(edge_in[d], d) for d in range(4)]
@@ -229,14 +223,14 @@
     row8 = iota((8, PAIR), 0)
     packed = sums + pltpu.roll(pltpu.roll(sums, 64, 1), 5, 0)
     out1[...] = packed[0:3]
-    hear(2)
+    hear(0)
     send_all(out1, lambda i: z1_in.at[i, pl.ds(0, 3)], z_peers, 0)
     wide1 = sign_live * basis
     signed3 = jnp.concatenate(
         [part for k in range(3) for part in (wide1[8 * k : 8 * k + 8], weight * wide1[8 * k : 8 * k + 8])], axis=0
     )
-    hear(5)
-    tell(6)
+    hear(3)
+    tell(4)
     loads[1].wait()
     loads[4].wait()
     spread_row, spread_col = iota((512, 384), 0), iota((512, 384), 1)
@@ -252,7 +246,7 @@
     for i in range(NSUB - 1):
         total = total + z1_in[i, pl.ds(0, 3), :]
     g1[c, pl.ds(0, 3), :] = total
-    hear(6)
+    hear(4)
     mine1 = g1.at[c, pl.ds(0, 3)]
     send_all(mine1, lambda i: mine1, clusters, 1)
     rest1 = g1.at[pl.ds(0, NCL - 1), pl.ds(0, 3)]
@@ -293,37 +287,47 @@
     image_sums = nt(signed3, image)
     scalars = nt(ones, jnp.concatenate([0.5 * projected * direction, operand * image], axis=0))
     lanes2 = join([image_sums[8 * k : 8 * k + 8] for k in range(6)] + [scalars])
-    out2[...] = lanes2[0:6]
-    send_all(out2, lambda i: z2_in.at[i, pl.ds(0, 6)], z_peers, 3)
+    lane8, sixth = iota((8, PAIR), 1), jnp.broadcast_to(lanes2[5:6], (8, PAIR))
+    for row in range(3):
+        here = (row8 == row) & (lane8 >= 96)
+        lanes2 = jnp.where(here, pltpu.roll(sixth, 96 - 32 * row, 1), lanes2)
+    out2[...] = lanes2[0:5]
+    send_all(out2, lambda i: z2_in.at[i, pl.ds(0, 5)], z_peers, 3)
     for d in range(4):
         halo[d] = image[:, d * PAIR : (d + 1) * PAIR]
     image_copies = halo_copies(halo, halo_in, 1)
     for copy in image_copies:
         copy.start()
-    whole(z2_in.at[:, pl.ds(0, 6)], 3, z_peers[0]).wait_recv()
+    whole(z2_in.at[:, pl.ds(0, 5)], 3, z_peers[0]).wait_recv()
     total = out2[...]
     for i in range(NSUB - 1):
-        total = total + z2_in[i, pl.ds(0, 6), :]
-    g2[c, pl.ds(0, 6), :] = total
-    mine2 = g2.at[c, pl.ds(0, 6)]
+        total = total + z2_in[i, pl.ds(0, 5), :]
+    g2[c, pl.ds(0, 5), :] = total
+    mine2 = g2.at[c, pl.ds(0, 5)]
     send_all(mine2, lambda i: mine2, clusters, 4)
     for copy in image_copies:
         copy.wait_recv()
     applied = sign_live * (image - join([partner_rows(halo_in[d], d) for d in range(4)]))
-    rest2 = g2.at[pl.ds(0, NCL - 1), pl.ds(0, 6)]
+    rest2 = g2.at[pl.ds(0, NCL - 1), pl.ds(0, 5)]
     whole(rest2, 4, clusters[0]).wait_recv()
 
     parts = [
-        jnp.concatenate([g2[k, pl.ds(0, 6), :], jnp.zeros((2, PAIR), F32)], axis=0) for k in range(NCL)
+        jnp.concatenate([g2[k, pl.ds(0, 5), :], jnp.zeros((3, PAIR), F32)], axis=0) for k in range(NCL)
     ]
     shifted = []
+    last_mode = (row8 == 5) & (lane8 < 32)
     for k in range(NCL):
+        last = jnp.broadcast_to(g2[k, pl.ds(1, 1), :], (8, PAIR))
+        if k + 1 < NCL:
+            last = last + jnp.broadcast_to(g2[k + 1, pl.ds(0, 1), :], (8, PAIR))
+        if k > 0:
+            last = last + jnp.broadcast_to(g2[k - 1, pl.ds(2, 1), :], (8, PAIR))
         x = pltpu.roll(parts[k], PAIR - 32, 1)
         if k + 1 < NCL:
             x = x + parts[k + 1]
         if k > 0:
             x = x + pltpu.roll(parts[k - 1], PAIR - 64, 1)
-        shifted.append(x)
+        shifted.append(jnp.where(last_mode, pltpu.roll(last, 32, 1), x))
     sums_all = parts[0]
     for k in range(1, NCL):
         sums_all = sums_all + parts[k]
@@ -332,7 +336,7 @@
         pick = jnp.where(iota((count * CASES, PAIR), 1) == iota((count * CASES, PAIR), 0) + start, 1.0, 0.0)
         return full_dot(pick.astype(F32), jnp.broadcast_to(row, (PAIR, PAIR)), ((1,), (1,)))
 
-    both = column(sums_all[0:1], 96, 2)
+    both = column(sums_all[3:4], 96, 2)
     rho, curve = both[0:CASES], both[CASES:]
     step = tile4(rho / curve)
     projected_f, direction_f = project(applied, solve(jnp.concatenate(shifted, axis=0)))
@@ -391,7 +395,7 @@
         copy.wait_send()
     whole(z1_in.at[:, pl.ds(0, 3)], 0, z_peers[0]).wait_send()
     whole(rest1, 1, clusters[0]).wait_send()
-    whole(z2_in.at[:, pl.ds(0, 6)], 3, z_peers[0]).wait_send()
+    whole(z2_in.at[:, pl.ds(0, 5)], 3, z_peers[0]).wait_send()
     whole(rest2, 4, clusters[0]).wait_send()
     whole(z3_in, 6, column_peers[0]).wait_send()
     whole(x3_in, 7, plane[0]).wait_send()
@@ -427,7 +431,7 @@
             pltpu.VMEM((3, PAIR), F32),
             pltpu.VMEM((NSUB - 1, 8, PAIR), F32),
             pltpu.VMEM((NCL, 8, PAIR), F32),
-            pltpu.VMEM((6, PAIR), F32),
+            pltpu.VMEM((5, PAIR), F32),
             pltpu.VMEM((NSUB - 1, 8, PAIR), F32),
             pltpu.VMEM((NCL, 8, PAIR), F32),
             pltpu.VMEM((1, PAIR), F32),
@@ -439,7 +443,7 @@
             pltpu.SemaphoreType.DMA((3, 4)),
             pltpu.SemaphoreType.DMA((9,)),
             pltpu.SemaphoreType.DMA((9,)),
-            pltpu.SemaphoreType.REGULAR((7,)),
+            pltpu.SemaphoreType.REGULAR((5,)),
         ],
         compiler_params=pltpu.CompilerParams(
             collective_id=0, has_side_effects=True, vmem_limit_bytes=60 * 1024*1024

time: 72.5 us -> 70.3 us (0.970)
  Pallas kernels: 70.2 us -> 68 us
    pallas_call x1, Pallas kernels: 70.2 us -> 68 us  [shards(): pl.pallas_call(kernel, out_shape=(terms_out, step_out, step_out), in_spec...]
where the time goes in v5:
time: 70.3 us; the launch traced here: 70.1 us
  Pallas kernels  68 us (97%)
  other arithmetic  1.48 us (2%)
    pallas_call x1, Pallas kernels, shards(): pl.pallas_call(kernel, out_shape=(terms_out, step_out, step_out), in_spec...  68 us
    add x1, other arithmetic, shards(): terms[0, k] + step[None] * terms[1, k] + older[None] * terms[2, k]  1.48 us

profile of v5, /device:TPU:1, one launch (start us, length us, event | category | flops | bytes accessed | tf_op | source)
XLA Modules:
  0.0 70.1 jit_solution(15717367927087143092)
XLA Ops:
  0.6 68.0 %feti.1 = (f32[3,2,4,16,128]{4,3,2,1,0:T(8,128)}, f32[16,128]{1,0:T(8,128)}, f32[16,128]{1,0:T(8,128)}) custom-call(bf16[1,1,512,512]{3,2,1,0:T(8,128)(2,1)} %schur_ref.1, f32[1,1,4,16,128]{4,3,2,1,0:T(8,128)} %load_ref.1, f32[1,1,6,4,128]{4,3,2,1,0:T(4,128)} %bitcast.1, s32[1,1,4]{2,1,0:T(1,128)} %len_ref.1, s32[1,1,4,128]{3,2,1,0:T(4,128)} %partner_ref.1, ...), custom_call_target="tpu_custom_call" | custom-call | tf_op jit(solution)/shard_map/feti/pallas_call | solution.py:409
  68.6 1.5 %multiply_add_fusion = (f32[1,1,4,16,128]{4,3,2,1,0:T(8,128)}, f32[1,1,4,16,128]{4,3,2,1,0:T(8,128)}) fusion(f32[3,2,4,16,128]{4,3,2,1,0:T(8,128)} %get-tuple-element.5, f32[16,128]{1,0:T(8,128)} %get-tuple-element.7, f32[16,128]{1,0:T(8,128)} %get-tuple-element.6), kind=kLoop, calls=%fused_computation | loop fusion | flops 65536 | bytes 278528 | tf_op jit(solution)/shard_map/add | solution.py:454

commit v6 on v5

--- a/solution.py
+++ b/solution.py
@@ -334,7 +334,7 @@
 
     def column(row, start, count):
         pick = jnp.where(iota((count * CASES, PAIR), 1) == iota((count * CASES, PAIR), 0) + start, 1.0, 0.0)
-        return full_dot(pick.astype(F32), jnp.broadcast_to(row, (PAIR, PAIR)), ((1,), (1,)))
+        return nt(pick.astype(F32), jnp.broadcast_to(row, (PAIR, PAIR)))
 
     both = column(sums_all[3:4], 96, 2)
     rho, curve = both[0:CASES], both[CASES:]

time: 70.3 us -> 70.2 us (level)
  no operation moved by 1% of the time
where the time goes in v6:
time: 70.2 us; the launch traced here: 69.9 us
  Pallas kernels  67.8 us (97%)
  other arithmetic  1.48 us (2%)
    pallas_call x1, Pallas kernels, shards(): pl.pallas_call(kernel, out_shape=(terms_out, step_out, step_out), in_spec...  67.8 us
    add x1, other arithmetic, shards(): terms[0, k] + step[None] * terms[1, k] + older[None] * terms[2, k]  1.48 us

profile of v6, /device:TPU:1, one launch (start us, length us, event | category | flops | bytes accessed | tf_op | source)
XLA Modules:
  0.0 69.9 jit_solution(18054507929244150758)
XLA Ops:
  0.6 67.8 %feti.1 = (f32[3,2,4,16,128]{4,3,2,1,0:T(8,128)}, f32[16,128]{1,0:T(8,128)}, f32[16,128]{1,0:T(8,128)}) custom-call(bf16[1,1,512,512]{3,2,1,0:T(8,128)(2,1)} %schur_ref.1, f32[1,1,4,16,128]{4,3,2,1,0:T(8,128)} %load_ref.1, f32[1,1,6,4,128]{4,3,2,1,0:T(4,128)} %bitcast.1, s32[1,1,4]{2,1,0:T(1,128)} %len_ref.1, s32[1,1,4,128]{3,2,1,0:T(4,128)} %partner_ref.1, ...), custom_call_target="tpu_custom_call" | custom-call | tf_op jit(solution)/shard_map/feti/pallas_call | solution.py:409
  68.4 1.5 %multiply_add_fusion = (f32[1,1,4,16,128]{4,3,2,1,0:T(8,128)}, f32[1,1,4,16,128]{4,3,2,1,0:T(8,128)}) fusion(f32[3,2,4,16,128]{4,3,2,1,0:T(8,128)} %get-tuple-element.5, f32[16,128]{1,0:T(8,128)} %get-tuple-element.7, f32[16,128]{1,0:T(8,128)} %get-tuple-element.6), kind=kLoop, calls=%fused_computation | loop fusion | flops 65536 | bytes 278528 | tf_op jit(solution)/shard_map/add | solution.py:454
